TPU v7x, 128 devices: a whole 4x4x4 slice. The times are simulated.
128 devices in a mesh: dp: 16 (over y_hi, z, core), blk: 8 (over x, y_lo).
Axes of the slice: x: 4, y: 4 (y_hi: 2, y_lo: 2; y = y_hi * 2 + y_lo), z: 4, core: 2. Of those that a mesh axis runs over, the one named last changes fastest.
Arguments:
- layer_input: bfloat16 [16, 1024, 768], P('dp', 'blk'), may hold values from -6 to 6
- out_grad: bfloat16 [16, 1024, 768], P('dp', 'blk'), may hold values from -6 to 6
- lengths: int32 [16, 4], P('dp'), may hold values from 3 to 1015, as said below
- keep: int32 [2, 16, 4], P(None, 'dp'), may hold values 0 or 1
- ln1_gain: float32 [768], replicated, may hold values from 0.5 to 1.5
- ln1_bias: float32 [768], replicated, may hold values from -3 to 3
- w_qkv: bfloat16 [768, 2304], replicated, may hold values from -0.21875 to 0.21875
- b_query: float32 [768], replicated, may hold values from -3 to 3
- b_value: float32 [768], replicated, may hold values from -3 to 3
- w_proj: bfloat16 [768, 768], replicated, may hold values from -1.25 to 1.25
- b_proj: float32 [768], replicated, may hold values from -2 to 2
- ln2_gain: float32 [768], replicated, may hold values from 0.5 to 1.5
- ln2_bias: float32 [768], replicated, may hold values from -3 to 3
- w_fc1: bfloat16 [768, 3072], replicated, may hold values from -0.21875 to 0.21875
- b_fc1: float32 [3072], replicated, may hold values from -3 to 3
- w_fc2: bfloat16 [3072, 768], replicated, may hold values from -0.109375 to 0.109375
- b_fc2: float32 [768], replicated, may hold values from -2 to 2
Outputs:
- output: bfloat16 [16, 1024, 768], P('dp', 'blk')
- x_grad: bfloat16 [16, 1024, 768], P('dp', 'blk')
- grad_ln1_gain: float32 [768], replicated
- grad_ln1_bias: float32 [768], replicated
- grad_w_qkv: float32 [768, 2304], replicated
- grad_b_query: float32 [768], replicated
- grad_b_value: float32 [768], replicated
- grad_w_proj: float32 [768, 768], replicated
- grad_b_proj: float32 [768], replicated
- grad_ln2_gain: float32 [768], replicated
- grad_ln2_bias: float32 [768], replicated
- grad_w_fc1: float32 [768, 3072], replicated
- grad_b_fc1: float32 [3072], replicated
- grad_w_fc2: float32 [3072, 768], replicated
- grad_b_fc2: float32 [768], replicated
Inputs may be any that keep to these rules, and one draw needn't show every extreme that they name: Each row holds 4 images of 3 or more tokens laid out in order from the row's start; their lengths sum to at most 1024, the remaining tokens are padding.
All inputs are finite; a program needn't handle non-finite values. No bound on the sum of `keep` on one device may be relied on, other than what follows from the above.
Results may differ from a plain program's by a relative error of at most 0.014.
Values may be sent and summed in bfloat16 or wider, within the bound.
No kernel may reach another device: no remote copies, remote signals or barrier semaphores. Data moves between devices by JAX's collectives and lax.ppermute only.
A program may use at most 192 MiB of HBM per device.

v0:
```python
import math

import jax
import jax.numpy as jnp
from jax import lax
from jax.sharding import PartitionSpec as P

D = 768
HEADS = 12
HEAD_DIM = 64
IMGS = 4


eps_norm = 1e-06
drop_scale = 1.0 / 0.9
far_below = -1e30
inv_root_two = 1.0 / math.sqrt(2.0)
inv_root_tau = 1.0 / math.sqrt(2.0 * math.pi)


def from_behind(block, axis, distance):
    devices = range(lax.axis_size(axis))
    route = [((i - distance) % len(devices), i) for i in devices]
    return lax.ppermute(block, axis, route)


def normalize(values):
    mean = jnp.mean(values, axis=-1, keepdims=True)
    centred = values - mean
    inverse = lax.rsqrt(jnp.mean(centred * centred, axis=-1, keepdims=True) + eps_norm)
    return (centred * inverse, inverse)


def norm_back(grad_out, normed, inverse, gain):
    scaled = grad_out * gain
    inner = (
        scaled
        - jnp.mean(scaled, axis=-1, keepdims=True)
        - normed * jnp.mean(scaled * normed, axis=-1, keepdims=True)
    )
    return (inverse * inner, jnp.sum(grad_out * normed, axis=0), jnp.sum(grad_out, axis=0))


def image_ids(ends, places):
    return jnp.sum((ends[:, None, :] <= places[None, :, None]).astype(jnp.int32), axis=2)


def split_heads(block):
    return block.reshape(block.shape[0], block.shape[1], HEADS, HEAD_DIM)


def front_part(x_float, ln1_gain, ln1_bias, w_qkv, qkv_bias):
    normed, inverse = normalize(x_float)
    h_one = (normed * ln1_gain + ln1_bias).astype(jnp.bfloat16)
    qkv = (jnp.dot(h_one, w_qkv, preferred_element_type=jnp.float32) + qkv_bias).astype(
        jnp.bfloat16
    )
    return (normed, inverse, h_one, qkv)


def middle_part(x_float, attended, scale_attn, w_proj, b_proj, ln2_gain, ln2_bias, w_fc1, b_fc1):
    branch = jnp.dot(attended, w_proj, preferred_element_type=jnp.float32) + b_proj
    mid = x_float + scale_attn[:, None] * branch
    normed, inverse = normalize(mid)
    h_two = (normed * ln2_gain + ln2_bias).astype(jnp.bfloat16)
    hidden = jnp.dot(h_two, w_fc1, preferred_element_type=jnp.float32) + b_fc1
    gelled = jax.nn.gelu(hidden, approximate=False).astype(jnp.bfloat16)
    return (mid, normed, inverse, h_two, hidden, gelled)


def block_scores(query, keys, query_ids, key_ids):
    scores = jnp.einsum(
        "rqhe,rkhe->rhqk", query, keys, preferred_element_type=jnp.float32
    ) * HEAD_DIM ** (-0.5)
    allowed = query_ids[:, None, :, None] == key_ids[:, None, None, :]
    return (scores, allowed)


def forward_step(carry, query, query_ids, piece, key_ids):
    top, total, accum = carry
    keys = split_heads(piece[:, :, :D])
    values = split_heads(piece[:, :, D:])
    scores, allowed = block_scores(query, keys, query_ids, key_ids)
    scores = jnp.where(allowed, scores, far_below)
    new_top = jnp.maximum(top, jnp.max(scores, axis=-1))
    weights = jnp.where(allowed, jnp.exp(scores - new_top[..., None]), 0.0)
    factor = jnp.exp(top - new_top)
    total = total * factor + jnp.sum(weights, axis=-1)
    update = jnp.einsum(
        "rhqk,rkhe->rhqe", weights.astype(jnp.bfloat16), values, preferred_element_type=jnp.float32
    )
    return (new_top, total, accum * factor[..., None] + update)


def backward_step(query, query_ids, log_total, grad_out, delta, piece, key_ids):
    keys = split_heads(piece[:, :, :D])
    values = split_heads(piece[:, :, D:])
    scores, allowed = block_scores(query, keys, query_ids, key_ids)
    probs = jnp.where(allowed, jnp.exp(scores - log_total[..., None]), 0.0)
    grad_probs = jnp.einsum("rqhe,rkhe->rhqk", grad_out, values, preferred_element_type=jnp.float32)
    grad_scores = (probs * (grad_probs - delta[..., None])).astype(jnp.bfloat16)
    factor = HEAD_DIM ** (-0.5)
    grad_query = (
        jnp.einsum("rhqk,rkhe->rqhe", grad_scores, keys, preferred_element_type=jnp.float32)
        * factor
    )
    grad_keys = (
        jnp.einsum("rhqk,rqhe->rkhe", grad_scores, query, preferred_element_type=jnp.float32)
        * factor
    )
    grad_values = jnp.einsum(
        "rhqk,rqhe->rkhe", probs.astype(jnp.bfloat16), grad_out, preferred_element_type=jnp.float32
    )
    rows_here, count_here = (piece.shape[0], piece.shape[1])
    term = jnp.concatenate(
        [
            grad_keys.reshape(rows_here, count_here, D),
            grad_values.reshape(rows_here, count_here, D),
        ],
        axis=-1,
    )
    return (grad_query, term)


def per_device(
    layer_input,
    out_grad,
    lengths,
    keep,
    ln1_gain,
    ln1_bias,
    w_qkv,
    b_query,
    b_value,
    w_proj,
    b_proj,
    ln2_gain,
    ln2_bias,
    w_fc1,
    b_fc1,
    w_fc2,
    b_fc2,
):
    rows, tokens, width = layer_input.shape
    count = rows * tokens
    cycle_size = lax.axis_size("blk")
    place = lax.axis_index("blk")
    ends = jnp.cumsum(lengths, axis=1)
    local_places = jnp.arange(tokens, dtype=jnp.int32)
    own_ids = image_ids(ends, place * tokens + local_places)
    valid = (own_ids < IMGS).astype(jnp.float32).reshape(count)
    onehot = (own_ids[:, :, None] == jnp.arange(IMGS, dtype=jnp.int32)[None, None, :]).astype(
        jnp.float32
    )
    keeps = jnp.einsum("rti,bri->brt", onehot, keep.astype(jnp.float32)) * drop_scale
    scale_attn = keeps[0].reshape(count)
    scale_mlp = keeps[1].reshape(count)
    qkv_bias = jnp.concatenate([b_query, jnp.zeros_like(b_query), b_value])
    x_float = layer_input.reshape(count, width).astype(jnp.float32) * valid[:, None]
    normed_one, inverse_one, h_one, qkv = front_part(x_float, ln1_gain, ln1_bias, w_qkv, qkv_bias)
    query = qkv[:, :width].reshape(rows, tokens, HEADS, HEAD_DIM)
    pairs = qkv[:, width:].reshape(rows, tokens, 2 * width)
    start_state = (
        jnp.full((rows, HEADS, tokens), far_below, jnp.float32),
        jnp.zeros((rows, HEADS, tokens), jnp.float32),
        jnp.zeros((rows, HEADS, tokens, HEAD_DIM), jnp.float32),
    )
    first = forward_step(start_state, query, own_ids, pairs, own_ids)

    def cycle_turn(step, state):
        moving, carry = state
        moving = from_behind(moving, "blk", 1)
        source = (place - step) % cycle_size
        key_ids = image_ids(ends, source * tokens + local_places)
        return (moving, forward_step(carry, query, own_ids, moving, key_ids))

    moved, (top, total, accum) = lax.fori_loop(1, cycle_size, cycle_turn, (pairs, first))
    log_total = top + jnp.log(total)
    attended_float = jnp.transpose(accum / total[..., None], (0, 2, 1, 3))
    attended = attended_float.reshape(count, width).astype(jnp.bfloat16)
    mid, normed_two, inverse_two, h_two, hidden, gelled = middle_part(
        x_float, attended, scale_attn, w_proj, b_proj, ln2_gain, ln2_bias, w_fc1, b_fc1
    )
    mlp_out = jnp.dot(gelled, w_fc2, preferred_element_type=jnp.float32) + b_fc2
    output = (mid + scale_mlp[:, None] * mlp_out).astype(jnp.bfloat16).reshape(rows, tokens, width)
    saved_x, saved_attended = lax.optimization_barrier((x_float, attended))
    normed_one, inverse_one, h_one, qkv = front_part(saved_x, ln1_gain, ln1_bias, w_qkv, qkv_bias)
    mid, normed_two, inverse_two, h_two, hidden, gelled = middle_part(
        saved_x, saved_attended, scale_attn, w_proj, b_proj, ln2_gain, ln2_bias, w_fc1, b_fc1
    )
    query = qkv[:, :width].reshape(rows, tokens, HEADS, HEAD_DIM)
    pairs = qkv[:, width:].reshape(rows, tokens, 2 * width)
    grad_z = out_grad.reshape(count, width).astype(jnp.float32)
    grad_mlp = (scale_mlp[:, None] * grad_z).astype(jnp.bfloat16)
    grad_w_fc2 = jnp.einsum("nf,nd->fd", gelled, grad_mlp, preferred_element_type=jnp.float32)
    grad_b_fc2 = jnp.sum(grad_mlp.astype(jnp.float32), axis=0)
    grad_gelled = jnp.einsum("nd,fd->nf", grad_mlp, w_fc2, preferred_element_type=jnp.float32)
    cumulative = 0.5 * (1.0 + lax.erf(hidden * inv_root_two))
    density = jnp.exp(-0.5 * hidden * hidden) * inv_root_tau
    grad_hidden = (grad_gelled * (cumulative + hidden * density)).astype(jnp.bfloat16)
    grad_w_fc1 = jnp.einsum("nd,nf->df", h_two, grad_hidden, preferred_element_type=jnp.float32)
    grad_b_fc1 = jnp.sum(grad_hidden.astype(jnp.float32), axis=0)
    grad_h_two = jnp.einsum("nf,df->nd", grad_hidden, w_fc1, preferred_element_type=jnp.float32)
    grad_mid_norm, grad_ln2_gain, grad_ln2_bias = norm_back(
        grad_h_two, normed_two, inverse_two, ln2_gain
    )
    grad_mid = grad_z + grad_mid_norm
    mlp_terms = (grad_ln2_gain, grad_ln2_bias, grad_w_fc1, grad_b_fc1, grad_w_fc2, grad_b_fc2)
    mlp_sums = mlp_terms
    grad_branch = (scale_attn[:, None] * grad_mid).astype(jnp.bfloat16)
    grad_w_proj = jnp.einsum(
        "nc,nd->cd", saved_attended, grad_branch, preferred_element_type=jnp.float32
    )
    grad_b_proj = jnp.sum(grad_branch.astype(jnp.float32), axis=0)
    grad_out = jnp.einsum(
        "nd,cd->nc", grad_branch, w_proj, preferred_element_type=jnp.float32
    ).astype(jnp.bfloat16)
    grad_out = grad_out.reshape(rows, tokens, HEADS, HEAD_DIM)
    delta = jnp.einsum("rqhe,rqhe->rhq", grad_out.astype(jnp.float32), attended_float)
    zero_query = jnp.zeros((rows, tokens, HEADS, HEAD_DIM), jnp.float32)

    def back_turn(step, state):
        moving, sums, grad_query = state
        source = (place - step) % cycle_size
        key_ids = image_ids(ends, source * tokens + local_places)
        query_term, term = backward_step(
            query, own_ids, log_total, grad_out, delta, moving, key_ids
        )
        sums = sums + term
        moving = from_behind(moving, "blk", 1)
        sums = from_behind(sums.astype(jnp.bfloat16), "blk", 1).astype(sums.dtype)
        return (moving, sums, grad_query + query_term)

    start_sums = jnp.zeros((rows, tokens, 2 * width), jnp.float32)
    moved, grad_pairs, grad_query = lax.fori_loop(
        0, cycle_size, back_turn, (pairs, start_sums, zero_query)
    )
    grad_qkv = jnp.concatenate(
        [grad_query.reshape(count, width), grad_pairs.reshape(count, 2 * width)], axis=1
    ).astype(jnp.bfloat16)
    grad_w_qkv = jnp.einsum("nd,nc->dc", h_one, grad_qkv, preferred_element_type=jnp.float32)
    column_sums = jnp.sum(grad_qkv.astype(jnp.float32), axis=0)
    grad_b_query = column_sums[:width]
    grad_b_value = column_sums[2 * width :]
    grad_h_one = jnp.einsum("nc,dc->nd", grad_qkv, w_qkv, preferred_element_type=jnp.float32)
    grad_x_norm, grad_ln1_gain, grad_ln1_bias = norm_back(
        grad_h_one, normed_one, inverse_one, ln1_gain
    )
    x_grad = (
        ((grad_mid + grad_x_norm) * valid[:, None])
        .astype(jnp.bfloat16)
        .reshape(rows, tokens, width)
    )
    summed = lax.psum(
        (
            grad_ln1_gain,
            grad_ln1_bias,
            grad_w_qkv,
            grad_b_query,
            grad_b_value,
            grad_w_proj,
            grad_b_proj,
            mlp_sums[0],
            mlp_sums[1],
            mlp_sums[2],
            mlp_sums[3],
            mlp_sums[4],
            mlp_sums[5],
        ),
        ("dp", "blk"),
    )
    attn_sums = summed[:7]
    mlp_sums = summed[7:]
    return (
        output,
        x_grad,
        attn_sums[0],
        attn_sums[1],
        attn_sums[2],
        attn_sums[3],
        attn_sums[4],
        attn_sums[5],
        attn_sums[6],
        mlp_sums[0],
        mlp_sums[1],
        mlp_sums[2],
        mlp_sums[3],
        mlp_sums[4],
        mlp_sums[5],
    )


def solution(mesh):
    placed = (
        P("dp", "blk", None),
        P("dp", "blk", None),
        P("dp", None),
        P(None, "dp", None),
        P(),
        P(),
        P(),
        P(),
        P(),
        P(),
        P(),
        P(),
        P(),
        P(),
        P(),
        P(),
        P(),
    )
    return jax.shard_map(
        per_device,
        mesh=mesh,
        in_specs=placed,
        out_specs=(
            P("dp", "blk", None),
            P("dp", "blk", None),
            P(),
            P(),
            P(),
            P(),
            P(),
            P(),
            P(),
            P(),
            P(),
            P(),
            P(),
            P(),
            P(),
        ),
        check_vma=False,
    )
```

profile of v0, /device:TPU:1, one launch (start us, length us, event | category | flops | bytes accessed | tf_op | source)
XLA Modules:
  0.0 632.8 jit_solution(6292684436855254632)
XLA Ops:
  16.2 1.9 copy.59
  29.2 105.1 %while.42 = (s32[]{:T(128)}, bf16[1,128,1536]{1,2,0:T(8,128)(2,1)}, f32[1,12,128]{2,1,0:T(8,128)S(1)}, f32[1,12,128]{2,1,0:T(8,128)S(1)}, f32[1,12,128,64]{2,3,1...) while((s32[]{:T(128)}, bf16[1,128,1536]{1,2,0:T(8,128)(2,1)}, ...), condition=%wide.region_10.11_spmd.clone, body=%wide.region_6.10_spmd.clone.sunk | while | flops 52320272 | bytes 10193790 | solution.py:177
  29.2 2.1 collective-permute-start
  32.9 9.5 %collective-permute-done = bf16[1,128,1536]{1,2,0:T(8,128)(2,1)} collective-permute-done((bf16[1,128,1536]{1,2,0:T(8,128)(2,1)}, bf16[1,128,1536]{1,2,0:T(8,128)(2,1)}, u32[]{:S(2)}, u32[]{:S(2)}) %collective-permute-start) | collective-permute-done | bytes 393248 | tf_op jit(solution)/shard_map/while/body/eval_jaxpr/ppermute | solution.py:24
  45.2 1.9 copy.86
  48.6 9.9 %collective-permute-done = bf16[1,128,1536]{1,2,0:T(8,128)(2,1)} collective-permute-done((bf16[1,128,1536]{1,2,0:T(8,128)(2,1)}, bf16[1,128,1536]{1,2,0:T(8,128)(2,1)}, u32[]{:S(2)}, u32[]{:S(2)}) %collective-permute-start) | collective-permute-done | bytes 393248 | tf_op jit(solution)/shard_map/while/body/eval_jaxpr/ppermute | solution.py:24
  61.4 1.9 copy.86
  64.9 9.0 %collective-permute-done = bf16[1,128,1536]{1,2,0:T(8,128)(2,1)} collective-permute-done((bf16[1,128,1536]{1,2,0:T(8,128)(2,1)}, bf16[1,128,1536]{1,2,0:T(8,128)(2,1)}, u32[]{:S(2)}, u32[]{:S(2)}) %collective-permute-start) | collective-permute-done | bytes 393248 | tf_op jit(solution)/shard_map/while/body/eval_jaxpr/ppermute | solution.py:24
  76.7 1.9 copy.86
  80.1 8.1 %collective-permute-done = bf16[1,128,1536]{1,2,0:T(8,128)(2,1)} collective-permute-done((bf16[1,128,1536]{1,2,0:T(8,128)(2,1)}, bf16[1,128,1536]{1,2,0:T(8,128)(2,1)}, u32[]{:S(2)}, u32[]{:S(2)}) %collective-permute-start) | collective-permute-done | bytes 393248 | tf_op jit(solution)/shard_map/while/body/eval_jaxpr/ppermute | solution.py:24
  91.1 1.9 copy.86
  94.5 7.5 %collective-permute-done = bf16[1,128,1536]{1,2,0:T(8,128)(2,1)} collective-permute-done((bf16[1,128,1536]{1,2,0:T(8,128)(2,1)}, bf16[1,128,1536]{1,2,0:T(8,128)(2,1)}, u32[]{:S(2)}, u32[]{:S(2)}) %collective-permute-start) | collective-permute-done | bytes 393248 | tf_op jit(solution)/shard_map/while/body/eval_jaxpr/ppermute | solution.py:24
  104.8 1.9 copy.86
  108.3 7.5 %collective-permute-done = bf16[1,128,1536]{1,2,0:T(8,128)(2,1)} collective-permute-done((bf16[1,128,1536]{1,2,0:T(8,128)(2,1)}, bf16[1,128,1536]{1,2,0:T(8,128)(2,1)}, u32[]{:S(2)}, u32[]{:S(2)}) %collective-permute-start) | collective-permute-done | bytes 393248 | tf_op jit(solution)/shard_map/while/body/eval_jaxpr/ppermute | solution.py:24
  118.6 1.9 copy.86
  122.1 7.5 %collective-permute-done = bf16[1,128,1536]{1,2,0:T(8,128)(2,1)} collective-permute-done((bf16[1,128,1536]{1,2,0:T(8,128)(2,1)}, bf16[1,128,1536]{1,2,0:T(8,128)(2,1)}, u32[]{:S(2)}, u32[]{:S(2)}) %collective-permute-start) | collective-permute-done | bytes 393248 | tf_op jit(solution)/shard_map/while/body/eval_jaxpr/ppermute | solution.py:24
  144.2 2.0 fusion.234
  146.5 3.3 convolution_add_fusion.2
  149.9 2.4 convert_reduce_fusion.2
  152.3 2.3 multiply_reduce_fusion
  159.3 7.0 %fusion.67 = f32[3072,768]{1,0:T(8,128)} fusion(f32[128,3072]{1,0:T(8,128)S(1)} %convolution_add_fusion.2, bf16[1,128,768]{2,1,0:T(8,128)(2,1)S(1)} %copy-done.23, f32[128]{0:T(128)S(1)} %get-tuple-element.757), kind=kOutput, calls=%fused_computation.114 | convolution fusion | flops 629833728 | bytes 11207168 | tf_op jit(solution)/shard_map/nf,nd->fd/dot_general | solution.py:195
  166.3 5.2 fusion.226
  172.2 1.9 copy.63
  178.7 164.2 %while.43 = (s32[]{:T(128)}, bf16[1,128,1536]{1,2,0:T(8,128)(2,1)}, f32[1,128,1536]{1,2,0:T(8,128)}, f32[1,128,12,64]{1,3,2,0:T(8,128)}, s32[1,128]{1,0:T(1,128)...) while((s32[]{:T(128)}, bf16[1,128,1536]{1,2,0:T(8,128)(2,1)}, ...), condition=%wide.region_21.22_spmd.clone, body=%wide.region_19.21_spmd.clone.sunk | while | flops 128599568 | bytes 21505192 | solution.py:235
  185.1 2.2 fusion.312
  187.3 6.9 %collective-permute-done.2 = bf16[1,128,1536]{1,2,0:T(8,128)(2,1)} collective-permute-done((bf16[1,128,1536]{1,2,0:T(8,128)(2,1)}, bf16[1,128,1536]{1,2,0:T(8,128)(2,1)}, u32[]{:S(2)}, u32[]{:S(2)}) %collective-permute-start.2) | collective-permute-done | bytes 393248 | tf_op jit(solution)/shard_map/while/body/eval_jaxpr/ppermute | solution.py:24
  194.2 1.9 convert_element_type.292
  196.1 2.7 collective-permute-done.1
  204.9 2.3 fusion.312
  207.2 6.7 %collective-permute-done.2 = bf16[1,128,1536]{1,2,0:T(8,128)(2,1)} collective-permute-done((bf16[1,128,1536]{1,2,0:T(8,128)(2,1)}, bf16[1,128,1536]{1,2,0:T(8,128)(2,1)}, u32[]{:S(2)}, u32[]{:S(2)}) %collective-permute-start.2) | collective-permute-done | bytes 393248 | tf_op jit(solution)/shard_map/while/body/eval_jaxpr/ppermute | solution.py:24
  214.0 1.9 convert_element_type.292
  215.9 2.3 collective-permute-done.1
  224.3 2.3 fusion.312
  226.6 6.7 %collective-permute-done.2 = bf16[1,128,1536]{1,2,0:T(8,128)(2,1)} collective-permute-done((bf16[1,128,1536]{1,2,0:T(8,128)(2,1)}, bf16[1,128,1536]{1,2,0:T(8,128)(2,1)}, u32[]{:S(2)}, u32[]{:S(2)}) %collective-permute-start.2) | collective-permute-done | bytes 393248 | tf_op jit(solution)/shard_map/while/body/eval_jaxpr/ppermute | solution.py:24
  233.3 1.9 convert_element_type.292
  235.3 2.3 collective-permute-done.1
  243.6 2.3 fusion.312
  246.0 6.7 %collective-permute-done.2 = bf16[1,128,1536]{1,2,0:T(8,128)(2,1)} collective-permute-done((bf16[1,128,1536]{1,2,0:T(8,128)(2,1)}, bf16[1,128,1536]{1,2,0:T(8,128)(2,1)}, u32[]{:S(2)}, u32[]{:S(2)}) %collective-permute-start.2) | collective-permute-done | bytes 393248 | tf_op jit(solution)/shard_map/while/body/eval_jaxpr/ppermute | solution.py:24
  252.7 1.9 convert_element_type.292
  254.6 2.3 collective-permute-done.1
  263.0 2.3 fusion.312
  265.3 7.2 %collective-permute-done.2 = bf16[1,128,1536]{1,2,0:T(8,128)(2,1)} collective-permute-done((bf16[1,128,1536]{1,2,0:T(8,128)(2,1)}, bf16[1,128,1536]{1,2,0:T(8,128)(2,1)}, u32[]{:S(2)}, u32[]{:S(2)}) %collective-permute-start.2) | collective-permute-done | bytes 393248 | tf_op jit(solution)/shard_map/while/body/eval_jaxpr/ppermute | solution.py:24
  272.6 1.9 convert_element_type.292
  274.5 2.3 collective-permute-done.1
  282.9 2.3 fusion.312
  285.2 8.3 %collective-permute-done.2 = bf16[1,128,1536]{1,2,0:T(8,128)(2,1)} collective-permute-done((bf16[1,128,1536]{1,2,0:T(8,128)(2,1)}, bf16[1,128,1536]{1,2,0:T(8,128)(2,1)}, u32[]{:S(2)}, u32[]{:S(2)}) %collective-permute-start.2) | collective-permute-done | bytes 393248 | tf_op jit(solution)/shard_map/while/body/eval_jaxpr/ppermute | solution.py:24
  293.5 1.9 convert_element_type.292
  295.5 2.3 collective-permute-done.1
  303.8 2.3 fusion.312
  306.2 9.4 %collective-permute-done.2 = bf16[1,128,1536]{1,2,0:T(8,128)(2,1)} collective-permute-done((bf16[1,128,1536]{1,2,0:T(8,128)(2,1)}, bf16[1,128,1536]{1,2,0:T(8,128)(2,1)}, u32[]{:S(2)}, u32[]{:S(2)}) %collective-permute-start.2) | collective-permute-done | bytes 393248 | tf_op jit(solution)/shard_map/while/body/eval_jaxpr/ppermute | solution.py:24
  315.6 1.9 convert_element_type.292
  317.5 2.3 collective-permute-done.1
  325.9 2.3 fusion.312
  328.2 10.5 %collective-permute-done.2 = bf16[1,128,1536]{1,2,0:T(8,128)(2,1)} collective-permute-done((bf16[1,128,1536]{1,2,0:T(8,128)(2,1)}, bf16[1,128,1536]{1,2,0:T(8,128)(2,1)}, u32[]{:S(2)}, u32[]{:S(2)}) %collective-permute-start.2) | collective-permute-done | bytes 393248 | tf_op jit(solution)/shard_map/while/body/eval_jaxpr/ppermute | solution.py:24
  338.7 1.9 convert_element_type.292
  340.6 2.3 collective-permute-done.1
  346.0 4.2 fusion.155
  352.2 3.9 multiply_reduce_fusion.1
  356.1 82.2 %all-reduce = (f32[768]{0:T(1024)}, f32[768]{0:T(1024)}, f32[768]{0:T(1024)}, f32[768]{0:T(1024)}, f32[768]{0:T(1024)}, /*index=5*/f32[768]{0:T(1024)}, f32[768]{0:T(1024)}, f32[3072]{0:T(1024)}, f32[768]{0:T(1024)}) all-reduce(f32[768]{0:T(1024)} %get-tuple-element.677, ...), channel_id=1, replica_groups=mesh['dp'=16,'blk'=8] {'dp','blk'}, use_global_device_ids=true, to_apply=%region_25.26 | all-reduce | flops 9216 | bytes 73728 | tf_op jit(solution)/shard_map/psum | solution.py:254
  442.8 9.6 %fusion.65 = bf16[1,128,768]{2,1,0:T(8,128)(2,1)} fusion(f32[128,768]{1,0:T(8,128)} %copy-done.16, bf16[3072,768]{1,0:T(8,128)(2,1)} %param.36, bf16[768,3072]{1,0:T(8,128)(2,1)} %param.34, f32[3072]{0:T(1024)} %param.35, f32[768]{0:T(1024)} %param.37, f32[768]{0:T(1024)S(1)} %copy-done.27, f32[768]{0:T(1024)S(1)} %copy-done.21, f32[128]{0:T(128)} %add_rsqrt_fusion.2, ...), kind=kOutput, calls=%fused_computation.111 | convolution fusion | flops 1234796544 | bytes 10050048 | tf_op jit(solution)/shard_map/dot_general | solution.py:184
  452.4 152.5 %all-reduce.4.cloned.1.call-done = (f32[768,2304]{1,0:T(8,128)}, f32[768,768]{1,0:T(8,128)}, f32[768,3072]{1,0:T(8,128)}, f32[3072,768]{1,0:T(8,128)}) async-done(((f32[768,2304]{1,0:T(8,128)}, f32[768,768]{1,0:T(8,128)}, f32[768,3072]{1,0:T(8,128)}, f32[3072,768]{1,0:T(8,128)}), (f32[768,2304]{1,0:T(8,128)}, f32[768,768]{1,0:T(8,128)}, f32[768,3072]{1,0:T(8,128)}, ...) | async-done | bytes 28311568 | tf_op jit(solution)/shard_map/psum | solution.py:254
  604.9 6.6 %copy.106 = f32[768,2304]{1,0:T(8,128)} copy(f32[768,2304]{1,0:T(8,128)} %get-tuple-element.1003) | data formatting | bytes 14155776
  612.9 9.3 %copy.108 = f32[768,3072]{1,0:T(8,128)} copy(f32[768,3072]{1,0:T(8,128)} %get-tuple-element.1010) | data formatting | bytes 18874368
  622.2 3.7 copy.109
  (484 shorter events, 130.5 us)
Async XLA Ops:
  7.2 5.9 copy-start
  7.2 597.7 %all-reduce.4.cloned.1.call-start = ((), (), s32[]{:S(2)}) async-start(), calls=%async_computation | async-start | bytes 56623104 | tf_op jit(solution)/shard_map/psum | solution.py:254
  9.4 15.8 %copy-start.19 = (pred[128,128]{0,1:T(8,128)(4,1)}, pred[128,128]{0,1:T(8,128)(4,1)S(1)}, u32[]{:S(2)}) copy-start(pred[128,128]{0,1:T(8,128)(4,1)S(1)} %broadcast_compare_fusion.2) | copy-start | bytes 49156
  29.2 13.2 %collective-permute-start = (bf16[1,128,1536]{1,2,0:T(8,128)(2,1)}, bf16[1,128,1536]{1,2,0:T(8,128)(2,1)}, u32[]{:S(2)}, u32[]{:S(2)}) collective-permute-start(bf16[1,128,1536]{1,2,0:T(8,128)(2,1)} %get-tuple-element.924), channel_id=1, source_target_pairs={{7,0},{0,1},{1,2},{2,3},{3,4},{4,5},{5,6},{6,7},{15,8},{8,9},{9,10... | collective-permute-start | bytes 1179656 | tf_op jit(solution)/shard_map/while/body/eval_jaxpr/ppermute | solution.py:24
  31.3 13.6 %copy-start.4 = (f32[1,12,128,64]{2,3,1,0:T(8,128)S(1)}, f32[1,12,128,64]{2,3,1,0:T(8,128)}, u32[]{:S(2)}) copy-start(f32[1,12,128,64]{2,3,1,0:T(8,128)} %get-tuple-element.927) | copy-start | bytes 1179652 | tf_op jit(solution)/shard_map/while
  47.1 11.5 %collective-permute-start = (bf16[1,128,1536]{1,2,0:T(8,128)(2,1)}, bf16[1,128,1536]{1,2,0:T(8,128)(2,1)}, u32[]{:S(2)}, u32[]{:S(2)}) collective-permute-start(bf16[1,128,1536]{1,2,0:T(8,128)(2,1)} %get-tuple-element.924), channel_id=1, source_target_pairs={{7,0},{0,1},{1,2},{2,3},{3,4},{4,5},{5,6},{6,7},{15,8},{8,9},{9,10... | collective-permute-start | bytes 1179656 | tf_op jit(solution)/shard_map/while/body/eval_jaxpr/ppermute | solution.py:24
  47.1 14.0 %copy-start.4 = (f32[1,12,128,64]{2,3,1,0:T(8,128)S(1)}, f32[1,12,128,64]{2,3,1,0:T(8,128)}, u32[]{:S(2)}) copy-start(f32[1,12,128,64]{2,3,1,0:T(8,128)} %get-tuple-element.927) | copy-start | bytes 1179652 | tf_op jit(solution)/shard_map/while
  63.3 10.6 %collective-permute-start = (bf16[1,128,1536]{1,2,0:T(8,128)(2,1)}, bf16[1,128,1536]{1,2,0:T(8,128)(2,1)}, u32[]{:S(2)}, u32[]{:S(2)}) collective-permute-start(bf16[1,128,1536]{1,2,0:T(8,128)(2,1)} %get-tuple-element.924), channel_id=1, source_target_pairs={{7,0},{0,1},{1,2},{2,3},{3,4},{4,5},{5,6},{6,7},{15,8},{8,9},{9,10... | collective-permute-start | bytes 1179656 | tf_op jit(solution)/shard_map/while/body/eval_jaxpr/ppermute | solution.py:24
  63.3 13.1 %copy-start.4 = (f32[1,12,128,64]{2,3,1,0:T(8,128)S(1)}, f32[1,12,128,64]{2,3,1,0:T(8,128)}, u32[]{:S(2)}) copy-start(f32[1,12,128,64]{2,3,1,0:T(8,128)} %get-tuple-element.927) | copy-start | bytes 1179652 | tf_op jit(solution)/shard_map/while
  78.6 9.6 %collective-permute-start = (bf16[1,128,1536]{1,2,0:T(8,128)(2,1)}, bf16[1,128,1536]{1,2,0:T(8,128)(2,1)}, u32[]{:S(2)}, u32[]{:S(2)}) collective-permute-start(bf16[1,128,1536]{1,2,0:T(8,128)(2,1)} %get-tuple-element.924), channel_id=1, source_target_pairs={{7,0},{0,1},{1,2},{2,3},{3,4},{4,5},{5,6},{6,7},{15,8},{8,9},{9,10... | collective-permute-start | bytes 1179656 | tf_op jit(solution)/shard_map/while/body/eval_jaxpr/ppermute | solution.py:24
  78.6 12.2 %copy-start.4 = (f32[1,12,128,64]{2,3,1,0:T(8,128)S(1)}, f32[1,12,128,64]{2,3,1,0:T(8,128)}, u32[]{:S(2)}) copy-start(f32[1,12,128,64]{2,3,1,0:T(8,128)} %get-tuple-element.927) | copy-start | bytes 1179652 | tf_op jit(solution)/shard_map/while
  93.0 9.1 %collective-permute-start = (bf16[1,128,1536]{1,2,0:T(8,128)(2,1)}, bf16[1,128,1536]{1,2,0:T(8,128)(2,1)}, u32[]{:S(2)}, u32[]{:S(2)}) collective-permute-start(bf16[1,128,1536]{1,2,0:T(8,128)(2,1)} %get-tuple-element.924), channel_id=1, source_target_pairs={{7,0},{0,1},{1,2},{2,3},{3,4},{4,5},{5,6},{6,7},{15,8},{8,9},{9,10... | collective-permute-start | bytes 1179656 | tf_op jit(solution)/shard_map/while/body/eval_jaxpr/ppermute | solution.py:24
  93.0 11.6 %copy-start.4 = (f32[1,12,128,64]{2,3,1,0:T(8,128)S(1)}, f32[1,12,128,64]{2,3,1,0:T(8,128)}, u32[]{:S(2)}) copy-start(f32[1,12,128,64]{2,3,1,0:T(8,128)} %get-tuple-element.927) | copy-start | bytes 1179652 | tf_op jit(solution)/shard_map/while
  106.7 9.1 %collective-permute-start = (bf16[1,128,1536]{1,2,0:T(8,128)(2,1)}, bf16[1,128,1536]{1,2,0:T(8,128)(2,1)}, u32[]{:S(2)}, u32[]{:S(2)}) collective-permute-start(bf16[1,128,1536]{1,2,0:T(8,128)(2,1)} %get-tuple-element.924), channel_id=1, source_target_pairs={{7,0},{0,1},{1,2},{2,3},{3,4},{4,5},{5,6},{6,7},{15,8},{8,9},{9,10... | collective-permute-start | bytes 1179656 | tf_op jit(solution)/shard_map/while/body/eval_jaxpr/ppermute | solution.py:24
  106.7 11.6 %copy-start.4 = (f32[1,12,128,64]{2,3,1,0:T(8,128)S(1)}, f32[1,12,128,64]{2,3,1,0:T(8,128)}, u32[]{:S(2)}) copy-start(f32[1,12,128,64]{2,3,1,0:T(8,128)} %get-tuple-element.927) | copy-start | bytes 1179652 | tf_op jit(solution)/shard_map/while
  120.5 9.1 %collective-permute-start = (bf16[1,128,1536]{1,2,0:T(8,128)(2,1)}, bf16[1,128,1536]{1,2,0:T(8,128)(2,1)}, u32[]{:S(2)}, u32[]{:S(2)}) collective-permute-start(bf16[1,128,1536]{1,2,0:T(8,128)(2,1)} %get-tuple-element.924), channel_id=1, source_target_pairs={{7,0},{0,1},{1,2},{2,3},{3,4},{4,5},{5,6},{6,7},{15,8},{8,9},{9,10... | collective-permute-start | bytes 1179656 | tf_op jit(solution)/shard_map/while/body/eval_jaxpr/ppermute | solution.py:24
  120.5 11.6 %copy-start.4 = (f32[1,12,128,64]{2,3,1,0:T(8,128)S(1)}, f32[1,12,128,64]{2,3,1,0:T(8,128)}, u32[]{:S(2)}) copy-start(f32[1,12,128,64]{2,3,1,0:T(8,128)} %get-tuple-element.927) | copy-start | bytes 1179652 | tf_op jit(solution)/shard_map/while
  142.7 3.8 copy-start.20
  142.7 3.8 copy-start.26
  142.7 3.8 copy-start.37
  144.2 10.4 %copy-start.42 = (f32[128]{0:T(128)}, f32[128]{0:T(128)S(1)}, u32[]{:S(2)}) copy-start(f32[128]{0:T(128)S(1)} %get-tuple-element.758) | copy-start | bytes 1540
  144.2 15.1 %copy-start.43 = (f32[128]{0:T(128)}, f32[128]{0:T(128)S(1)}, u32[]{:S(2)}) copy-start(f32[128]{0:T(128)S(1)} %get-tuple-element.757) | copy-start | bytes 1540
  144.2 5.7 copy-start.46
  146.5 5.8 slice-start
  179.0 3.6 copy-start.3
  185.1 9.1 %collective-permute-start.2 = (bf16[1,128,1536]{1,2,0:T(8,128)(2,1)}, bf16[1,128,1536]{1,2,0:T(8,128)(2,1)}, u32[]{:S(2)}, u32[]{:S(2)}) collective-permute-start(bf16[1,128,1536]{1,2,0:T(8,128)(2,1)} %fusion.311), channel_id=1, source_target_pairs={{7,0},{0,1},{1,2},{2,3},{3,4},{4,5},{5,6},{6,7},{15,8},{8,9},{9,10... | collective-permute-start | bytes 1179656 | tf_op jit(solution)/shard_map/while/body/eval_jaxpr/ppermute | solution.py:24
  185.1 13.7 %collective-permute-start.1 = (bf16[1,128,1536]{1,2,0:T(8,128)(2,1)}, bf16[1,128,1536]{1,2,0:T(8,128)(2,1)}, u32[]{:S(2)}, u32[]{:S(2)}) collective-permute-start(bf16[1,128,1536]{1,2,0:T(8,128)(2,1)} %copy.95), channel_id=1, source_target_pairs={{7,0},{0,1},{1,2},{2,3},{3,4},{4,5},{5,6},{6,7},{15,8},{8,9},{9,10... | collective-permute-start | bytes 1179656 | tf_op jit(solution)/shard_map/while/body/eval_jaxpr/ppermute | solution.py:24
  198.8 3.6 copy-start.3
  204.9 9.1 %collective-permute-start.2 = (bf16[1,128,1536]{1,2,0:T(8,128)(2,1)}, bf16[1,128,1536]{1,2,0:T(8,128)(2,1)}, u32[]{:S(2)}, u32[]{:S(2)}) collective-permute-start(bf16[1,128,1536]{1,2,0:T(8,128)(2,1)} %fusion.311), channel_id=1, source_target_pairs={{7,0},{0,1},{1,2},{2,3},{3,4},{4,5},{5,6},{6,7},{15,8},{8,9},{9,10... | collective-permute-start | bytes 1179656 | tf_op jit(solution)/shard_map/while/body/eval_jaxpr/ppermute | solution.py:24
  204.9 13.3 %collective-permute-start.1 = (bf16[1,128,1536]{1,2,0:T(8,128)(2,1)}, bf16[1,128,1536]{1,2,0:T(8,128)(2,1)}, u32[]{:S(2)}, u32[]{:S(2)}) collective-permute-start(bf16[1,128,1536]{1,2,0:T(8,128)(2,1)} %copy.95), channel_id=1, source_target_pairs={{7,0},{0,1},{1,2},{2,3},{3,4},{4,5},{5,6},{6,7},{15,8},{8,9},{9,10... | collective-permute-start | bytes 1179656 | tf_op jit(solution)/shard_map/while/body/eval_jaxpr/ppermute | solution.py:24
  218.2 3.6 copy-start.3
  224.3 9.1 %collective-permute-start.2 = (bf16[1,128,1536]{1,2,0:T(8,128)(2,1)}, bf16[1,128,1536]{1,2,0:T(8,128)(2,1)}, u32[]{:S(2)}, u32[]{:S(2)}) collective-permute-start(bf16[1,128,1536]{1,2,0:T(8,128)(2,1)} %fusion.311), channel_id=1, source_target_pairs={{7,0},{0,1},{1,2},{2,3},{3,4},{4,5},{5,6},{6,7},{15,8},{8,9},{9,10... | collective-permute-start | bytes 1179656 | tf_op jit(solution)/shard_map/while/body/eval_jaxpr/ppermute | solution.py:24
  224.3 13.3 %collective-permute-start.1 = (bf16[1,128,1536]{1,2,0:T(8,128)(2,1)}, bf16[1,128,1536]{1,2,0:T(8,128)(2,1)}, u32[]{:S(2)}, u32[]{:S(2)}) collective-permute-start(bf16[1,128,1536]{1,2,0:T(8,128)(2,1)} %copy.95), channel_id=1, source_target_pairs={{7,0},{0,1},{1,2},{2,3},{3,4},{4,5},{5,6},{6,7},{15,8},{8,9},{9,10... | collective-permute-start | bytes 1179656 | tf_op jit(solution)/shard_map/while/body/eval_jaxpr/ppermute | solution.py:24
  237.6 3.6 copy-start.3
  243.6 9.1 %collective-permute-start.2 = (bf16[1,128,1536]{1,2,0:T(8,128)(2,1)}, bf16[1,128,1536]{1,2,0:T(8,128)(2,1)}, u32[]{:S(2)}, u32[]{:S(2)}) collective-permute-start(bf16[1,128,1536]{1,2,0:T(8,128)(2,1)} %fusion.311), channel_id=1, source_target_pairs={{7,0},{0,1},{1,2},{2,3},{3,4},{4,5},{5,6},{6,7},{15,8},{8,9},{9,10... | collective-permute-start | bytes 1179656 | tf_op jit(solution)/shard_map/while/body/eval_jaxpr/ppermute | solution.py:24
  243.6 13.3 %collective-permute-start.1 = (bf16[1,128,1536]{1,2,0:T(8,128)(2,1)}, bf16[1,128,1536]{1,2,0:T(8,128)(2,1)}, u32[]{:S(2)}, u32[]{:S(2)}) collective-permute-start(bf16[1,128,1536]{1,2,0:T(8,128)(2,1)} %copy.95), channel_id=1, source_target_pairs={{7,0},{0,1},{1,2},{2,3},{3,4},{4,5},{5,6},{6,7},{15,8},{8,9},{9,10... | collective-permute-start | bytes 1179656 | tf_op jit(solution)/shard_map/while/body/eval_jaxpr/ppermute | solution.py:24
  256.9 3.6 copy-start.3
  263.0 9.6 %collective-permute-start.2 = (bf16[1,128,1536]{1,2,0:T(8,128)(2,1)}, bf16[1,128,1536]{1,2,0:T(8,128)(2,1)}, u32[]{:S(2)}, u32[]{:S(2)}) collective-permute-start(bf16[1,128,1536]{1,2,0:T(8,128)(2,1)} %fusion.311), channel_id=1, source_target_pairs={{7,0},{0,1},{1,2},{2,3},{3,4},{4,5},{5,6},{6,7},{15,8},{8,9},{9,10... | collective-permute-start | bytes 1179656 | tf_op jit(solution)/shard_map/while/body/eval_jaxpr/ppermute | solution.py:24
  263.0 13.8 %collective-permute-start.1 = (bf16[1,128,1536]{1,2,0:T(8,128)(2,1)}, bf16[1,128,1536]{1,2,0:T(8,128)(2,1)}, u32[]{:S(2)}, u32[]{:S(2)}) collective-permute-start(bf16[1,128,1536]{1,2,0:T(8,128)(2,1)} %copy.95), channel_id=1, source_target_pairs={{7,0},{0,1},{1,2},{2,3},{3,4},{4,5},{5,6},{6,7},{15,8},{8,9},{9,10... | collective-permute-start | bytes 1179656 | tf_op jit(solution)/shard_map/while/body/eval_jaxpr/ppermute | solution.py:24
  276.8 3.6 copy-start.3
  282.9 10.6 %collective-permute-start.2 = (bf16[1,128,1536]{1,2,0:T(8,128)(2,1)}, bf16[1,128,1536]{1,2,0:T(8,128)(2,1)}, u32[]{:S(2)}, u32[]{:S(2)}) collective-permute-start(bf16[1,128,1536]{1,2,0:T(8,128)(2,1)} %fusion.311), channel_id=1, source_target_pairs={{7,0},{0,1},{1,2},{2,3},{3,4},{4,5},{5,6},{6,7},{15,8},{8,9},{9,10... | collective-permute-start | bytes 1179656 | tf_op jit(solution)/shard_map/while/body/eval_jaxpr/ppermute | solution.py:24
  282.9 14.9 %collective-permute-start.1 = (bf16[1,128,1536]{1,2,0:T(8,128)(2,1)}, bf16[1,128,1536]{1,2,0:T(8,128)(2,1)}, u32[]{:S(2)}, u32[]{:S(2)}) collective-permute-start(bf16[1,128,1536]{1,2,0:T(8,128)(2,1)} %copy.95), channel_id=1, source_target_pairs={{7,0},{0,1},{1,2},{2,3},{3,4},{4,5},{5,6},{6,7},{15,8},{8,9},{9,10... | collective-permute-start | bytes 1179656 | tf_op jit(solution)/shard_map/while/body/eval_jaxpr/ppermute | solution.py:24
  297.8 3.6 copy-start.3
  303.8 11.7 %collective-permute-start.2 = (bf16[1,128,1536]{1,2,0:T(8,128)(2,1)}, bf16[1,128,1536]{1,2,0:T(8,128)(2,1)}, u32[]{:S(2)}, u32[]{:S(2)}) collective-permute-start(bf16[1,128,1536]{1,2,0:T(8,128)(2,1)} %fusion.311), channel_id=1, source_target_pairs={{7,0},{0,1},{1,2},{2,3},{3,4},{4,5},{5,6},{6,7},{15,8},{8,9},{9,10... | collective-permute-start | bytes 1179656 | tf_op jit(solution)/shard_map/while/body/eval_jaxpr/ppermute | solution.py:24
  303.8 15.9 %collective-permute-start.1 = (bf16[1,128,1536]{1,2,0:T(8,128)(2,1)}, bf16[1,128,1536]{1,2,0:T(8,128)(2,1)}, u32[]{:S(2)}, u32[]{:S(2)}) collective-permute-start(bf16[1,128,1536]{1,2,0:T(8,128)(2,1)} %copy.95), channel_id=1, source_target_pairs={{7,0},{0,1},{1,2},{2,3},{3,4},{4,5},{5,6},{6,7},{15,8},{8,9},{9,10... | collective-permute-start | bytes 1179656 | tf_op jit(solution)/shard_map/while/body/eval_jaxpr/ppermute | solution.py:24
  319.8 3.6 copy-start.3
  325.9 12.8 %collective-permute-start.2 = (bf16[1,128,1536]{1,2,0:T(8,128)(2,1)}, bf16[1,128,1536]{1,2,0:T(8,128)(2,1)}, u32[]{:S(2)}, u32[]{:S(2)}) collective-permute-start(bf16[1,128,1536]{1,2,0:T(8,128)(2,1)} %fusion.311), channel_id=1, source_target_pairs={{7,0},{0,1},{1,2},{2,3},{3,4},{4,5},{5,6},{6,7},{15,8},{8,9},{9,10... | collective-permute-start | bytes 1179656 | tf_op jit(solution)/shard_map/while/body/eval_jaxpr/ppermute | solution.py:24
  325.9 17.0 %collective-permute-start.1 = (bf16[1,128,1536]{1,2,0:T(8,128)(2,1)}, bf16[1,128,1536]{1,2,0:T(8,128)(2,1)}, u32[]{:S(2)}, u32[]{:S(2)}) collective-permute-start(bf16[1,128,1536]{1,2,0:T(8,128)(2,1)} %copy.95), channel_id=1, source_target_pairs={{7,0},{0,1},{1,2},{2,3},{3,4},{4,5},{5,6},{6,7},{15,8},{8,9},{9,10... | collective-permute-start | bytes 1179656 | tf_op jit(solution)/shard_map/while/body/eval_jaxpr/ppermute | solution.py:24
  352.1 4.0 copy-start.31
  352.1 4.0 copy-start.32
  352.1 86.2 %copy-start.30 = (f32[768]{0:T(1024)S(1)}, f32[768]{0:T(1024)}, u32[]{:S(2)}) copy-start(f32[768]{0:T(1024)} %param.31) | copy-start | bytes 9220
  438.3 3.5 copy-start.49
  438.3 3.5 copy-start.7
  438.3 3.5 copy-start.15
  438.4 3.5 copy-start.18
  438.4 3.5 copy-start.35
  438.4 3.5 copy-start.36
  438.4 3.5 copy-start.40
  438.4 4.4 copy-start.21
  438.4 4.4 copy-start.27
  604.9 6.6 %copy-start.13 = (f32[768,768]{1,0:T(8,128)S(1)}, f32[768,768]{1,0:T(8,128)}, u32[]{:S(2)}) copy-start(f32[768,768]{1,0:T(8,128)} %get-tuple-element.1006) | copy-start | bytes 7077892
  611.4 10.7 %slice-start.2 = ((s8[9437184]{0:T(1024)(128)(4,1)}), s8[4194304]{0:T(1024)(128)(4,1)S(1)}, s32[]{:S(2)}) async-start(s8[9437184]{0:T(1024)(128)(4,1)} %bitcast.233), calls=%async_computation.3 | async-start | bytes 8388608
  612.9 9.3 %slice-start.3 = ((s8[9437184]{0:T(1024)(128)(4,1)}), s8[4194304]{0:T(1024)(128)(4,1)S(1)}, s32[]{:S(2)}) async-start(s8[9437184]{0:T(1024)(128)(4,1)} %bitcast.233), calls=%async_computation.4 | async-start | bytes 8388608
  612.9 9.3 %slice-start.4 = ((s8[9437184]{0:T(1024)(128)(4,1)}), s8[1048576]{0:T(1024)(128)(4,1)S(1)}, s32[]{:S(2)}) async-start(s8[9437184]{0:T(1024)(128)(4,1)} %bitcast.233), calls=%async_computation.5 | async-start | bytes 2097152
  (84 other events, 181.5 us)
Sparse Core Ops, SparseCore 0:
  350.4 254.4 all-reduce.3
where the time goes:
time: 635 us; the launch traced here: 633 us
  waiting for transfers between devices  293 us (46%)
  matrix products  92 us (14%)
  local copies, waits for them, and re-layouts  90.9 us (14%)
  blocking collectives  82.2 us (13%)
  other arithmetic  56.4 us (9%)
  between operations  14.6 us (2%)
    psum x1, waiting for transfers between devices, per_device(): lax.psum((grad_ln1_gain, grad_ln1_bias, grad_w_qkv, grad_b_query, grad_b_...  152 us
    ppermute x23, waiting for transfers between devices, from_behind(): return lax.ppermute(block, axis, route)  140 us
    psum x1, blocking collectives, per_device(): lax.psum((grad_ln1_gain, grad_ln1_bias, grad_w_qkv, grad_b_query, grad_b_...  82.2 us
    while x178, local copies, waits for them, and re-layouts  34.3 us
    unnamed x98, local copies, waits for them, and re-layouts  26.9 us
    convert_element_type x16, other arithmetic, back_turn(): sums = from_behind(sums.astype(jnp.bfloat16), 'blk', 1).astype(sums.dtype)  22.1 us
    dot_general x8, matrix products, backward_step(): jnp.einsum('rhqk,rkhe->rqhe', grad_scores, keys, preferred_element_type=j...  18.4 us
    dot_general x16, matrix products, block_scores(): jnp.einsum('rqhe,rkhe->rhqk', query, keys, preferred_element_type=jnp.flo...  13.7 us
  transfers between devices with their start and end apart: 24, of which 24 were waited for; matrix products, arithmetic and copies ran while one was open for 10% of the time, Pallas kernels for 0%

commit v1 on v0

v1 whole, which is shorter than its diff:
```python
import math

import jax
import jax.numpy as jnp
from jax import lax
from jax.sharding import Mesh
from jax.sharding import PartitionSpec as P

D = 768
HEADS = 12
HEAD_DIM = 64
FF = 3072
IMGS = 4
TP = 8
COLS = D // TP
HID = FF // TP
PAIR = 2 * HEAD_DIM
VEC_ROWS = 16

eps_norm = 1e-06
drop_scale = 1.0 / 0.9
far_below = -1e30
inv_root_two = 1.0 / math.sqrt(2.0)
inv_root_tau = 1.0 / math.sqrt(2.0 * math.pi)

BLK = ("x", "yl")
bf16 = jnp.bfloat16
f32 = jnp.float32


def dot(a, b, dims):
    return lax.dot_general(a, b, ((dims[0], dims[1]), ((), ())), preferred_element_type=f32)


def normalize(values):
    mean = jnp.mean(values, axis=-1, keepdims=True)
    centred = values - mean
    inverse = lax.rsqrt(jnp.mean(centred * centred, axis=-1, keepdims=True) + eps_norm)
    return (centred * inverse, inverse)


def norm_back(grad_out, normed, inverse, gain):
    scaled = grad_out * gain
    inner = (
        scaled
        - jnp.mean(scaled, axis=-1, keepdims=True)
        - normed * jnp.mean(scaled * normed, axis=-1, keepdims=True)
    )
    return (inverse * inner, jnp.sum(grad_out * normed, axis=0), jnp.sum(grad_out, axis=0))


def spread(block, axes, count):
    tiled = jnp.broadcast_to(block[None], (count,) + block.shape)
    return lax.all_to_all(tiled, axes, 0, 0)


def exchange(block, axis, by_core):
    sizes = [2 if name in ("c", "yh", "yl") else 4 for name in axis]
    route = []
    for place in range(math.prod(sizes)):
        left, spots = place, {}
        for name, size in reversed(list(zip(axis, sizes))):
            left, spots[name] = divmod(left, size)
        mask = by_core[spots["c"]]
        if "yh" in spots:
            spots["yh"] ^= mask // 2
            spots["yl"] ^= mask % 2
        else:
            spots[axis[0] if axis[0] != "c" else axis[1]] ^= mask
        partner = 0
        for name, size in zip(axis, sizes):
            partner = partner * size + spots[name]
        route.append((place, partner))
    return lax.ppermute(block, axis, route)


def swap_core(block):
    return lax.ppermute(block, "c", [(0, 1), (1, 0)])


def sum_rows(partial, extra):
    core = lax.axis_index("c")
    halves = partial.reshape(2, HID, HID)
    mine = lax.dynamic_index_in_dim(halves, core, 0, keepdims=False)
    other = lax.dynamic_index_in_dim(halves, 1 - core, 0, keepdims=False)
    if extra is not None:
        mine = jnp.concatenate([mine, extra], axis=0)
        other = jnp.concatenate([other, extra], axis=0)
    got = swap_core(other.astype(bf16))
    half = (mine + got.astype(f32)).astype(bf16)
    pieces = half[:HID].reshape(8, HID // 8, HID)
    if extra is not None:
        tail = jnp.broadcast_to(half[HID:][None], (8, VEC_ROWS, HID))
        pieces = jnp.concatenate([pieces, tail], axis=1)
    pieces = lax.all_to_all(pieces, ("yh", "z"), 0, 0)
    return jnp.sum(pieces.astype(f32), axis=0).astype(bf16)


def double_twice(block, axis):
    one = exchange(block, axis, (1, 3))
    block = jnp.stack([block, one])
    two = exchange(block, axis, (3, 1))
    return jnp.concatenate([block, two])


def in_order(relative, place):
    core = lax.axis_index("c")
    first = jnp.array([0, 1, 3, 2], jnp.int32)
    second = jnp.array([0, 2, 3, 1], jnp.int32)
    table = jnp.where(core == 0, first, second)
    spots = [table[place ^ v] for v in range(4)]
    return jnp.stack([lax.dynamic_index_in_dim(relative, s, 0, keepdims=False) for s in spots])


def both_cores(block):
    core = lax.axis_index("c")
    got = swap_core(block)
    return jnp.stack([jnp.where(core == 0, block, got), jnp.where(core == 0, got, block)])


def per_device(
    layer_input,
    out_grad,
    lengths,
    keep,
    ln1_gain,
    ln1_bias,
    w_qkv,
    b_query,
    b_value,
    w_proj,
    b_proj,
    ln2_gain,
    ln2_bias,
    w_fc1,
    b_fc1,
    w_fc2,
    b_fc2,
):
    _, tokens, width = layer_input.shape
    row = tokens * TP
    group = lax.axis_index(BLK)
    ends = jnp.cumsum(lengths[0])
    places = jnp.arange(row, dtype=jnp.int32)
    ids = jnp.sum((ends[:, None] <= places[None, :]).astype(jnp.int32), axis=0)
    valid = (ids < IMGS).astype(f32)
    onehot = (ids[:, None] == jnp.arange(IMGS, dtype=jnp.int32)[None, :]).astype(f32)
    keeps = jnp.sum(onehot[None] * keep[:, 0, None, :].astype(f32), axis=2) * drop_scale
    here = group * tokens

    def own(v):
        return lax.dynamic_slice_in_dim(v, here, tokens, 0)

    own_ids = own(ids)
    scale_attn = own(keeps[0])[:, None]
    scale_mlp = own(keeps[1])[:, None]
    qkv_bias = jnp.concatenate([b_query, jnp.zeros_like(b_query), b_value])

    x_all = spread(layer_input[0], BLK, TP).reshape(row, width).astype(f32) * valid[:, None]
    normed_all, _ = normalize(x_all)
    h_all = (normed_all * ln1_gain + ln1_bias).astype(bf16)
    x_own = layer_input[0].astype(f32) * own(valid)[:, None]
    normed_one, inverse_one = normalize(x_own)
    h_own = (normed_one * ln1_gain + ln1_bias).astype(bf16)
    grad_z = out_grad[0].astype(f32)
    grad_mlp = (scale_mlp * grad_z).astype(bf16)
    grad_mlp_all = spread(grad_mlp, BLK, TP).reshape(row, width)

    query = (dot(h_own, w_qkv[:, :width], ((1,), (0,))) + b_query).astype(bf16)
    pairs = (dot(h_all, w_qkv[:, width:], ((1,), (0,))) + qkv_bias[width:]).astype(bf16)
    query = query.reshape(tokens, HEADS, HEAD_DIM)
    keys = pairs[:, :width].reshape(row, HEADS, HEAD_DIM)
    values = pairs[:, width:].reshape(row, HEADS, HEAD_DIM)
    scores = jnp.einsum("qhe,khe->hqk", query, keys, preferred_element_type=f32) * HEAD_DIM**-0.5
    allowed = own_ids[:, None] == ids[None, :]
    scores = jnp.where(allowed[None], scores, far_below)
    top = jnp.max(scores, axis=-1, keepdims=True)
    expo = jnp.exp(scores - top)
    probs = (expo / jnp.sum(expo, axis=-1, keepdims=True)).astype(bf16)
    attended = jnp.einsum("hqk,khe->qhe", probs, values, preferred_element_type=f32)
    attended = attended.reshape(tokens, width).astype(bf16)
    attended_all = spread(attended, BLK, TP).reshape(row, width)

    branch = dot(attended, w_proj, ((1,), (0,))) + b_proj
    mid = x_own + scale_attn * branch
    normed_two, inverse_two = normalize(mid)
    h_two = (normed_two * ln2_gain + ln2_bias).astype(bf16)
    hidden = dot(h_two, w_fc1, ((1,), (0,))) + b_fc1
    cumulative = 0.5 * (1.0 + lax.erf(hidden * inv_root_two))
    density = jnp.exp(-0.5 * hidden * hidden) * inv_root_tau
    gelled = (hidden * cumulative).astype(bf16)
    mlp_out = dot(gelled, w_fc2, ((1,), (0,))) + b_fc2
    output = (mid + scale_mlp * mlp_out).astype(bf16)
    grad_gelled = dot(grad_mlp, w_fc2, ((1,), (1,)))
    grad_hidden = (grad_gelled * (cumulative + hidden * density)).astype(bf16)
    grad_h_two = dot(grad_hidden, w_fc1, ((1,), (1,)))
    grad_mid_norm, ln2_gain_sum, ln2_bias_sum = norm_back(
        grad_h_two, normed_two, inverse_two, ln2_gain
    )
    grad_mid = grad_z + grad_mid_norm
    grad_branch = (scale_attn * grad_mid).astype(bf16)
    grad_att = dot(grad_branch, w_proj, ((1,), (1,))).astype(bf16)
    b_fc2_sum = jnp.sum(grad_mlp.astype(f32), axis=0)

    def first_head(j):
        return 3 * (j // 2) + j % 2

    outgoing = jnp.stack(
        [
            jnp.concatenate(
                [
                    grad_att[:, first_head(j) * HEAD_DIM :][:, :PAIR],
                    grad_branch[:, j * COLS : (j + 1) * COLS],
                    jnp.zeros((tokens, 2 * PAIR - PAIR - COLS), bf16),
                ],
                axis=1,
            )
            for j in range(TP)
        ]
    )
    incoming = lax.all_to_all(outgoing, BLK, 0, 0).reshape(row, 2 * PAIR)
    grad_att_pair = incoming[:, :PAIR]
    grad_branch_cols = incoming[:, PAIR : PAIR + COLS]

    start = first_head(group) * HEAD_DIM
    shift = (group % 2) * (HEAD_DIM // 2)
    w_pair = [
        lax.dynamic_slice(w_qkv, (0, t * width + start), (width, PAIR)) for t in range(3)
    ]
    bias_pair = [
        lax.dynamic_slice_in_dim(b_query, start, PAIR, 0),
        jnp.zeros((PAIR,), f32),
        lax.dynamic_slice_in_dim(b_value, start, PAIR, 0),
    ]
    qkv_pair = [
        (dot(h_all, w, ((1,), (0,))) + b).astype(bf16).reshape(row, 2, HEAD_DIM)
        for w, b in zip(w_pair, bias_pair)
    ]
    q2, k2, v2 = qkv_pair
    scores2 = jnp.einsum("qhe,khe->hqk", q2, k2, preferred_element_type=f32) * HEAD_DIM**-0.5
    allowed2 = ids[:, None] == ids[None, :]
    scores2 = jnp.where(allowed2[None], scores2, far_below)
    expo2 = jnp.exp(scores2 - jnp.max(scores2, axis=-1, keepdims=True))
    probs2 = expo2 / jnp.sum(expo2, axis=-1, keepdims=True)
    dob = grad_att_pair.reshape(row, 2, HEAD_DIM)
    dp2 = jnp.einsum("qhe,khe->hqk", dob, v2, preferred_element_type=f32)
    delta = jnp.sum(probs2 * dp2, axis=-1, keepdims=True)
    ds = (probs2 * (dp2 - delta)).astype(bf16)
    dq = jnp.einsum("hqk,khe->qhe", ds, k2, preferred_element_type=f32) * HEAD_DIM**-0.5
    dk = jnp.einsum("hqk,qhe->khe", ds, q2, preferred_element_type=f32) * HEAD_DIM**-0.5
    dv = jnp.einsum("hqk,qhe->khe", probs2.astype(bf16), dob, preferred_element_type=f32)
    parts = [
        lax.dynamic_slice(t.reshape(row, PAIR), (0, shift), (row, COLS)).astype(bf16)
        for t in (dq, dk, dv)
    ]
    dqkv = jnp.concatenate(parts, axis=1)
    dqkv_own = lax.all_to_all(dqkv.reshape(TP, tokens, 3 * COLS), BLK, 0, 0)
    w_cols = jnp.concatenate(
        [lax.dynamic_slice(w, (0, shift), (width, COLS)) for w in w_pair], axis=1
    )
    grad_h_cols = dot(dqkv, w_cols, ((1,), (1,)))
    ln1_gain_sum = jnp.sum(grad_h_cols * normed_all, axis=0)
    ln1_bias_sum = jnp.sum(grad_h_cols, axis=0)
    grad_b = jnp.concatenate(
        [dot(dqkv, h_all, ((0,), (0,))), dot(grad_branch_cols, attended_all, ((0,), (0,)))]
    )
    dqkv_sums = jnp.sum(dqkv.astype(f32), axis=0)
    b_proj_sum = jnp.sum(grad_branch_cols.astype(f32), axis=0)

    branch_all = dot(attended_all, w_proj, ((1,), (0,))) + b_proj
    mid_all = x_all + keeps[0][:, None] * branch_all
    h_two_all = (normalize(mid_all)[0] * ln2_gain + ln2_bias).astype(bf16)
    w_one = lax.dynamic_slice_in_dim(w_fc1, group * HID, HID, 1)
    w_two = lax.dynamic_slice_in_dim(w_fc2, group * HID, HID, 0)
    hid = dot(h_two_all, w_one, ((1,), (0,))) + lax.dynamic_slice_in_dim(b_fc1, group * HID, HID, 0)
    cumul = 0.5 * (1.0 + lax.erf(hid * inv_root_two))
    dens = jnp.exp(-0.5 * hid * hid) * inv_root_tau
    gel = (hid * cumul).astype(bf16)
    grad_hid = (dot(grad_mlp_all, w_two, ((1,), (1,))) * (cumul + hid * dens)).astype(bf16)
    grad_one = dot(h_two_all, grad_hid, ((0,), (0,)))
    grad_two = dot(gel, grad_mlp_all, ((0,), (0,)))
    b_fc1_sum = jnp.sum(grad_hid.astype(f32), axis=0)

    dqkv_rows = jnp.transpose(dqkv_own.reshape(TP, tokens, 3, COLS), (1, 2, 0, 3))
    grad_h_one = dot(dqkv_rows.reshape(tokens, 3 * width), w_qkv, ((1,), (1,)))
    grad_x_norm, _, _ = norm_back(grad_h_one, normed_one, inverse_one, ln1_gain)
    x_grad = ((grad_mid + grad_x_norm) * own(valid)[:, None]).astype(bf16)

    vec = jnp.concatenate(
        [
            ln1_gain_sum,
            ln1_bias_sum,
            ln2_gain_sum,
            ln2_bias_sum,
            b_fc2_sum,
            b_fc1_sum,
            dqkv_sums[:COLS],
            dqkv_sums[2 * COLS :],
            b_proj_sum,
            jnp.zeros((VEC_ROWS * HID - 11 * HID - 3 * COLS,), f32),
        ]
    ).reshape(VEC_ROWS, HID)

    def halves(m):
        return jnp.concatenate([m[:, :HID], m[:, HID:]], axis=0)

    piece_one = sum_rows(grad_one, None)
    piece_two = sum_rows(halves(grad_two), None)
    piece_b = sum_rows(halves(grad_b), vec)
    early_one = spread(piece_one, ("yh", "z", "yl"), 16)
    early_two = spread(piece_two, ("z", "x"), 16)
    early_b = spread(piece_b, ("yh", "x", "yl"), 16)
    vec_all = early_b.reshape(2, TP, HID // 8 + VEC_ROWS, HID)[0, :, HID // 8 :].astype(f32)
    early_b = early_b[:, : HID // 8]
    axis_x = ("c", "x")
    axis_y = ("yh", "c", "yl")
    axis_z = ("z", "c")
    whole_one = in_order(double_twice(early_one, axis_x), lax.axis_index("x"))
    whole_two = in_order(double_twice(early_two, axis_y), lax.axis_index(("yh", "yl")))
    whole_b = in_order(double_twice(early_b, axis_z), lax.axis_index("z"))
    one = both_cores(whole_one).reshape(2, 4, 2, 4, 2, HID // 8, HID)
    grad_w_fc1 = jnp.transpose(one, (0, 2, 3, 5, 1, 4, 6)).reshape(D, FF).astype(f32)
    two = both_cores(whole_two).reshape(2, 2, 2, 4, 4, HID // 8, HID)
    grad_w_fc2 = jnp.transpose(two, (4, 2, 1, 3, 5, 0, 6)).reshape(FF, D).astype(f32)
    b = both_cores(whole_b).reshape(2, 4, 2, TP, HID // 8, HID)
    b = jnp.transpose(b, (0, 5, 2, 1, 3, 4)).reshape(D, 4, 2, TP, HID // 8)
    b = jnp.transpose(b, (0, 1, 3, 2, 4)).reshape(D, 4 * D).astype(f32)
    flat = vec_all.reshape(TP, VEC_ROWS * HID)
    shared = jnp.sum(flat[:, : 5 * D], axis=0).reshape(5, D)
    tail = flat[:, 5 * D + HID :]
    return (
        output[None],
        x_grad[None],
        shared[0],
        shared[1],
        b[:, : 3 * D],
        tail[:, :COLS].reshape(D),
        tail[:, COLS : 2 * COLS].reshape(D),
        b[:, 3 * D :],
        tail[:, 2 * COLS : 3 * COLS].reshape(D),
        shared[2],
        shared[3],
        grad_w_fc1,
        flat[:, 5 * D : 5 * D + HID].reshape(FF),
        grad_w_fc2,
        shared[4],
    )


def solution(mesh):
    fine = Mesh(mesh.devices.reshape(2, 4, 2, 4, 2), ("yh", "z", "c", "x", "yl"))
    dp = ("yh", "z", "c")
    tokens = P(dp, BLK, None)
    placed = (tokens, tokens, P(dp, None), P(None, dp, None)) + (P(),) * 13
    return jax.shard_map(
        per_device,
        mesh=fine,
        in_specs=placed,
        out_specs=(tokens, tokens) + (P(),) * 13,
        check_vma=False,
    )
```

time: 635 us -> 460 us (0.72)
  the two profiles are of different devices: /device:TPU:1 before, /device:TPU:17 now
where the time goes in v1:
time: 460 us; the launch traced here: 451 us
  local copies, waits for them, and re-layouts  126 us (27%)
  starting transfers between devices  94 us (20%)
  matrix products  83 us (18%)
  other arithmetic  72.6 us (16%)
  waiting for transfers between devices  50.6 us (11%)
  between operations  25.5 us (6%)
    dot_general x19, matrix products, dot(): lax.dot_general(a, b, ((dims[0], dims[1]), ((), ())), preferred_element_t...  51 us
    all_to_all x6, starting transfers between devices, spread(): return lax.all_to_all(tiled, axes, 0, 0)  32.7 us
    all_to_all x6, waiting for transfers between devices, spread(): return lax.all_to_all(tiled, axes, 0, 0)  32.7 us
    ppermute x6, starting transfers between devices, swap_core(): return lax.ppermute(block, 'c', [(0, 1), (1, 0)])  26.2 us
    all_to_all x3, starting transfers between devices, sum_rows(): pieces = lax.all_to_all(pieces, ('yh', 'z'), 0, 0)  20.4 us
    unnamed x190, local copies, waits for them, and re-layouts  19.5 us
    convert_element_type x2, local copies, waits for them, and re-layouts, per_device(): jnp.transpose(one, (0, 2, 3, 5, 1, 4, 6)).reshape(D, FF).astype(f32)  19.1 us
    convert_element_type x2, local copies, waits for them, and re-layouts, per_device(): b = jnp.transpose(b, (0, 1, 3, 2, 4)).reshape(D, 4 * D).astype(f32)  17.6 us
  transfers between devices with their start and end apart: 23, of which 9 were waited for; matrix products, arithmetic and copies ran while one was open for 34% of the time, Pallas kernels for 0%

profile of v1, /device:TPU:17, one launch (start us, length us, event | category | flops | bytes accessed | tf_op | source)
XLA Modules:
  0.0 451.5 jit_solution(2910556070075614996)
XLA Ops:
  0.7 2.3 broadcast_in_dim.42
  3.0 4.7 %all-to-all-start = ((bf16[8,128,768]{2,1,0:T(8,128)(2,1)}), bf16[8,128,768]{2,1,0:T(8,128)(2,1)S(1)}, u32[]{:S(2)}, u32[]{:S(2)}) async-start(bf16[8,128,768]{2,1,0:T(8,128)(2,1)} %broadcast_in_dim.42), calls=%async_computation | async-start | bytes 3145728 | tf_op jit(solution)/shard_map/all_to_all | solution.py:54
  17.0 2.3 constant_dynamic-slice_fusion.14
  22.5 8.3 %all-to-all-done = bf16[8,128,768]{2,1,0:T(8,128)(2,1)S(1)} async-done(((bf16[8,128,768]{2,1,0:T(8,128)(2,1)}), bf16[8,128,768]{2,1,0:T(8,128)(2,1)S(1)}, u32[]{:S(2)}, u32[]{:S(2)}) %all-to-all-start) | async-done | bytes 1572896 | tf_op jit(solution)/shard_map/all_to_all | solution.py:54
  33.3 2.8 add_convert_fusion
  38.0 2.6 copy.114
  40.6 3.0 copy.116
  43.6 6.6 %fusion.128 = (f32[12,128]{1,0:T(8,128)S(1)}, f32[12,128,1024]{2,1,0:T(8,128)}) fusion(pred[128,1024]{1,0:T(8,128)(4,1)S(1)} %broadcast_compare_fusion.1, bf16[128,12,64]{0,2,1:T(8,128)(2,1)S(1)} %bitcast.269, bf16[1024,12,64]{0,2,1:T(8,128)(2,1)} %bitcast.253), kind=kOutput, calls=%fused_computation.261 | convolution fusion | flops 207619072 | bytes 8198144 | tf_op jit(solution)/shard_map/sub | solution.py:178
  50.2 4.7 %fusion.38 = bf16[12,64,128]{2,1,0:T(8,128)(2,1)S(1)} fusion(bf16[1024,12,64]{0,2,1:T(8,128)(2,1)} %bitcast.252, f32[12,128,1024]{2,1,0:T(8,128)} %get-tuple-element.173, f32[12,128]{1,0:T(8,128)S(1)} %get-tuple-element.172), kind=kOutput, calls=%fused_computation.98 | convolution fusion | flops 204570624 | bytes 8067072 | tf_op jit(solution)/shard_map/hqk,khe->qhe/dot_general | solution.py:180
  57.2 2.0 convolution_add_fusion
  59.2 8.7 %multiply_reduce_fusion.4 = (f32[768]{0:T(1024)}, f32[128]{0:T(128)}, f32[128]{0:T(128)}, f32[768]{0:T(1024)}, f32[128,768]{1,0:T(8,128)}) fusion(f32[128,768]{1,0:T(8,128)S(1)} %get-tuple-element.175, f32[128]{0:T(128)} %copy-done.76, f32[128]{0:T(128)} %copy-done.61, f32[768]{0:T(1024)S(1)} %copy-done.41, bf16[768,3072]{1,0:T(8,128)(2,1)} %param.36, ...), kind=kOutput, calls=%fused_computation.136 | convolution fusion | flops 1213069568 | bytes 12004864 | tf_op jit(solution)/shard_map/dot_general | solution.py:32
  69.3 2.6 multiply_convert_fusion.6
  73.3 2.4 convolution_convert_fusion
  88.8 4.3 all-to-all-start.1
  93.1 3.0 fusion.26
  96.2 2.4 fusion.27
  98.6 8.7 %fusion.132 = (f32[2,1024]{1,0:T(2,128)}, f32[2,1024,1024]{1,2,0:T(8,128)}) fusion(pred[1024,1024]{0,1:T(8,128)(4,1)} %broadcast_compare_fusion, bf16[1024,2,64]{0,2,1:T(8,128)(2,1)} %bitcast.256, bf16[1024,2,64]{0,2,1:T(8,128)(2,1)} %bitcast.248), kind=kOutput, calls=%fused_computation.263 | convolution fusion | flops 276825088 | bytes 9969664 | tf_op jit(solution)/shard_map/sub | solution.py:243
  108.5 5.2 %all-to-all-start.3 = ((bf16[8,128,768]{2,1,0:T(8,128)(2,1)}), bf16[8,128,768]{2,1,0:T(8,128)(2,1)}, u32[]{:S(2)}, u32[]{:S(2)}) async-start(bf16[8,128,768]{2,1,0:T(8,128)(2,1)} %broadcast_in_dim.49), calls=%async_computation.3 | async-start | bytes 3145728 | tf_op jit(solution)/shard_map/all_to_all | solution.py:54
  117.2 4.9 %fusion.4 = bf16[2,64,1024]{2,1,0:T(8,128)(2,1)S(1)} fusion(bf16[1024,2,64]{0,2,1:T(8,128)(2,1)} %bitcast.267, f32[2,1024,1024]{1,2,0:T(8,128)} %get-tuple-element.178, f32[2,1024]{1,0:T(2,128)S(1)} %copy-done.55), kind=kOutput, calls=%fused_computation.15 | convolution fusion | flops 272629760 | bytes 8921088 | tf_op jit(solution)/shard_map/hqk,qhe->khe/dot_general | solution.py:251
  122.2 4.9 %multiply_reduce_fusion = (f32[2,1024]{1,0:T(2,128)S(1)}, f32[2,1024,1024]{1,2,0:T(8,128)S(1)}) fusion(f32[2,1024,1024]{1,2,0:T(8,128)} %get-tuple-element.178, f32[2,1024]{1,0:T(2,128)S(1)} %copy-done.55, bf16[1024,2,64]{0,2,1:T(8,128)(2,1)S(1)} %bitcast.268, bf16[1024,2,64]{0,2,1:T(8,128)(2,1)S(1)} %bitcast.266), kind=kOutput, calls=%fused_computation.6 | convolution fusion | flops 274724864 | bytes 17317888 | tf_op jit(solution)/shard_map/qhe,khe->hqk/dot_general | solution.py:246
  128.0 2.4 multiply_convert_fusion
  137.8 3.2 fusion.116
  142.3 5.5 %all-to-all-start.4 = ((bf16[8,128,768]{2,1,0:T(8,128)(2,1)}), bf16[8,128,768]{2,1,0:T(8,128)(2,1)}, u32[]{:S(2)}, u32[]{:S(2)}) async-start(bf16[8,128,768]{2,1,0:T(8,128)(2,1)} %broadcast_in_dim.51), calls=%async_computation.4 | async-start | bytes 3145728 | tf_op jit(solution)/shard_map/all_to_all | solution.py:54
  147.9 3.0 fusion.133
  151.4 1.9 fusion.70
  155.0 3.2 convolution_add_fusion.1
  158.2 10.5 %all-to-all-done.4 = bf16[8,128,768]{2,1,0:T(8,128)(2,1)} async-done(((bf16[8,128,768]{2,1,0:T(8,128)(2,1)}), bf16[8,128,768]{2,1,0:T(8,128)(2,1)}, u32[]{:S(2)}, u32[]{:S(2)}) %all-to-all-start.4) | async-done | bytes 1572896 | tf_op jit(solution)/shard_map/all_to_all | solution.py:54
  168.8 4.2 all-to-all-start.2
  173.0 4.4 convert_reduce_fusion
  177.5 3.4 fusion.43
  182.0 2.5 collective-permute-start
  188.4 7.7 %all-to-all-start.7 = ((bf16[8,48,384]{2,1,0:T(8,128)(2,1)}), bf16[8,48,384]{2,1,0:T(8,128)(2,1)S(1)}, u32[]{:S(2)}, u32[]{:S(2)}) async-start(bf16[8,48,384]{2,1,0:T(8,128)(2,1)} %bitcast.255), calls=%async_computation.7 | async-start | bytes 589824 | tf_op jit(solution)/shard_map/all_to_all | solution.py:95
  198.7 2.5 all-to-all-done.7
  201.2 6.7 %all-to-all-start.9 = ((bf16[8,48,384]{2,1,0:T(8,128)(2,1)}), bf16[8,48,384]{2,1,0:T(8,128)(2,1)S(1)}, u32[]{:S(2)}, u32[]{:S(2)}) async-start(bf16[8,48,384]{2,1,0:T(8,128)(2,1)} %bitcast.77), calls=%async_computation.9 | async-start | bytes 589824 | tf_op jit(solution)/shard_map/all_to_all | solution.py:95
  210.0 3.1 all-to-all-done.9
  213.0 6.0 %all-to-all-start.5 = ((bf16[8,64,384]{2,1,0:T(8,128)(2,1)}), bf16[8,64,384]{2,1,0:T(8,128)(2,1)S(1)}, u32[]{:S(2)}, u32[]{:S(2)}) async-start(bf16[8,64,384]{2,1,0:T(8,128)(2,1)} %pad_maximum_fusion.12), calls=%async_computation.5 | async-start | bytes 786432 | tf_op jit(solution)/shard_map/all_to_all | solution.py:95
  219.0 5.9 %all-to-all-done.5 = bf16[8,64,384]{2,1,0:T(8,128)(2,1)S(1)} async-done(((bf16[8,64,384]{2,1,0:T(8,128)(2,1)}), bf16[8,64,384]{2,1,0:T(8,128)(2,1)S(1)}, u32[]{:S(2)}, u32[]{:S(2)}) %all-to-all-start.5) | async-done | bytes 393248 | tf_op jit(solution)/shard_map/all_to_all | solution.py:95
  225.8 5.7 %all-to-all-start.8 = ((bf16[16,48,384]{2,1,0:T(8,128)(2,1)}), bf16[16,48,384]{2,1,0:T(8,128)(2,1)S(1)}, u32[]{:S(2)}, u32[]{:S(2)}) async-start(bf16[16,48,384]{2,1,0:T(8,128)(2,1)} %broadcast_in_dim.55), calls=%async_computation.8 | async-start | bytes 1179648 | tf_op jit(solution)/shard_map/all_to_all | solution.py:54
  231.6 7.1 %all-to-all-done.8 = bf16[16,48,384]{2,1,0:T(8,128)(2,1)S(1)} async-done(((bf16[16,48,384]{2,1,0:T(8,128)(2,1)}), bf16[16,48,384]{2,1,0:T(8,128)(2,1)S(1)}, u32[]{:S(2)}, u32[]{:S(2)}) %all-to-all-start.8) | async-done | bytes 589856 | tf_op jit(solution)/shard_map/all_to_all | solution.py:54
  239.6 5.3 %all-to-all-start.10 = ((bf16[16,48,384]{2,1,0:T(8,128)(2,1)}), bf16[16,48,384]{2,1,0:T(8,128)(2,1)S(1)}, u32[]{:S(2)}, u32[]{:S(2)}) async-start(bf16[16,48,384]{2,1,0:T(8,128)(2,1)} %broadcast_in_dim.56), calls=%async_computation.10 | async-start | bytes 1179648 | tf_op jit(solution)/shard_map/all_to_all | solution.py:54
  244.9 2.6 collective-permute-start.5
  247.6 6.8 %all-to-all-done.10 = bf16[16,48,384]{2,1,0:T(8,128)(2,1)S(1)} async-done(((bf16[16,48,384]{2,1,0:T(8,128)(2,1)}), bf16[16,48,384]{2,1,0:T(8,128)(2,1)S(1)}, u32[]{:S(2)}, u32[]{:S(2)}) %all-to-all-start.10) | async-done | bytes 589856 | tf_op jit(solution)/shard_map/all_to_all | solution.py:54
  255.4 6.2 %all-to-all-start.6 = ((bf16[16,64,384]{2,1,0:T(8,128)(2,1)}), bf16[16,64,384]{2,1,0:T(8,128)(2,1)}, u32[]{:S(2)}, u32[]{:S(2)}) async-start(bf16[16,64,384]{2,1,0:T(8,128)(2,1)} %broadcast_in_dim.54), calls=%async_computation.6 | async-start | bytes 1572864 | tf_op jit(solution)/shard_map/all_to_all | solution.py:54
  285.9 2.2 pad_maximum_fusion.8
  289.8 3.9 fusion.39
  300.5 6.1 %collective-permute-done.1 = bf16[16,48,384]{2,1,0:T(8,128)(2,1)S(1)} collective-permute-done((bf16[16,48,384]{2,1,0:T(8,128)(2,1)S(1)}, bf16[16,48,384]{2,1,0:T(8,128)(2,1)S(1)}, u32[]{:S(2)}, u32[]{:S(2)}) %collective-permute-start.1) | collective-permute-done | bytes 589856 | tf_op jit(solution)/shard_map/ppermute | solution.py:74
  310.6 16.2 %collective-permute-start.7 = (bf16[4,16,48,384]{3,2,1,0:T(8,128)(2,1)}, bf16[4,16,48,384]{3,2,1,0:T(8,128)(2,1)}, u32[]{:S(2)}, u32[]{:S(2)}) collective-permute-start(bf16[4,16,48,384]{3,2,1,0:T(8,128)(2,1)} %pad_maximum_fusion.3), channel_id=1, source_target_pairs={{0,8},{8,0},{1,9},{9,1},{2,10},{10,2},{3,11},{11,3},{4,12},{12,4},... | collective-permute-start | bytes 7077896 | tf_op jit(solution)/shard_map/ppermute | solution.py:78
  332.0 2.0 pad_maximum_fusion.1
  333.9 6.5 %collective-permute-start.3 = (bf16[4,16,48,384]{3,2,1,0:T(8,128)(2,1)}, bf16[4,16,48,384]{3,2,1,0:T(8,128)(2,1)}, u32[]{:S(2)}, u32[]{:S(2)}) collective-permute-start(bf16[4,16,48,384]{3,2,1,0:T(8,128)(2,1)} %pad_maximum_fusion.1), channel_id=1, source_target_pairs={{0,8},{8,0},{1,9},{9,1},{2,10},{10,2},{3,11},{11,3},{4,12},{12,4},... | collective-permute-start | bytes 7077896 | tf_op jit(solution)/shard_map/ppermute | solution.py:78
  348.3 2.0 broadcast_select_fusion.3
  350.9 6.1 %copy.128 = f32[2,2,4,48,4,2,384]{6,5,4,3,2,1,0:T(2,128)} copy(f32[2,2,4,48,4,2,384]{6,3,5,2,1,4,0:T(8,128)S(1)} %convert_bitcast_fusion.2) | data formatting | bytes 18874368 | tf_op jit(solution)/shard_map/convert_element_type | solution.py:322
  357.0 13.0 %reshape.436 = f32[768,3072]{1,0:T(8,128)} reshape(f32[2,2,4,48,4,2,384]{6,5,4,3,2,1,0:T(2,128)} %copy.128) | data formatting | bytes 18874368 | tf_op jit(solution)/shard_map/convert_element_type | solution.py:322
  370.0 2.0 broadcast_select_fusion.1
  372.6 12.5 %copy.129 = f32[4,2,2,4,48,2,384]{6,5,4,3,2,1,0:T(2,128)S(1)} copy(f32[4,2,2,4,48,2,384]{6,4,0,3,1,2,5:T(8,128)S(1)} %convert_bitcast_fusion.1) | data formatting | bytes 18874368 | tf_op jit(solution)/shard_map/convert_element_type | solution.py:324
  385.1 4.4 copy.138
  389.5 3.2 broadcast_select_fusion.5
  392.7 7.9 %copy.126 = bf16[1,4,2,8,48,384]{5,0,4,3,1,2:T(2,128)(2,1)} copy(bf16[1,4,2,8,48,384]{5,4,3,2,1,0:T(8,128)(2,1)} %bitcast.228) | data formatting | bytes 4718592 | tf_op jit(solution)/shard_map/stack | solution.py:118
  400.6 6.3 %copy.125 = bf16[1,4,2,8,48,384]{5,0,4,3,1,2:T(2,128)(2,1)} copy(bf16[1,4,2,8,48,384]{5,4,3,2,1,0:T(8,128)(2,1)S(1)} %bitcast.227) | data formatting | bytes 4718592 | tf_op jit(solution)/shard_map/stack | solution.py:118
  406.8 13.4 %convert_bitcast_fusion = f32[2,384,2,4,8,48]{1,0,5,4,3,2:T(2,128)} fusion(bf16[1,4,2,8,48,384]{5,0,4,3,1,2:T(2,128)(2,1)} %copy.126, bf16[1,4,2,8,48,384]{5,0,4,3,1,2:T(2,128)(2,1)} %copy.125), kind=kLoop, calls=%fused_computation.2 | loop fusion | flops 9437184 | bytes 14155776 | tf_op jit(solution)/shard_map/convert_element_type | solution.py:327
  420.3 13.0 %reshape.438 = f32[768,4,2,8,48]{0,4,3,2,1:T(8,128)} reshape(f32[2,384,2,4,8,48]{1,0,5,4,3,2:T(2,128)} %convert_bitcast_fusion) | data formatting | bytes 18874368 | tf_op jit(solution)/shard_map/convert_element_type | solution.py:327
  433.3 4.6 %copy.127 = f32[768,4,8,2,48]{0,4,3,2,1:T(8,128)S(1)} copy(f32[768,4,8,2,48]{0,4,2,3,1:T(8,128)} %bitcast.225) | data formatting | bytes 18874368 | tf_op jit(solution)/shard_map/convert_element_type | solution.py:327
  437.8 3.3 slice.237
  441.3 8.1 %copy.130 = f32[768,2304]{1,0:T(8,128)} copy(f32[768,2304]{0,1:T(8,128)} %slice.237) | data formatting | bytes 14155776
  449.4 1.9 copy.131
  (337 shorter events, 91.3 us)
Async XLA Ops:
  0.6 55.0 %copy-start = (bf16[768,768]{1,0:T(8,128)(2,1)S(1)}, bf16[768,768]{1,0:T(8,128)(2,1)}, u32[]{:S(2)}) copy-start(bf16[768,768]{1,0:T(8,128)(2,1)} %param.32) | copy-start | bytes 3538948
  0.7 7.1 %copy-start.86 = (s32[1,4]{1,0:T(1,128)S(1)}, s32[1,4]{1,0:T(1,128)}, u32[]{:S(2)}) copy-start(s32[1,4]{1,0:T(1,128)} %param.25) | copy-start | bytes 52
  0.7 8.6 %copy-start.6 = (bf16[1,128,768]{2,1,0:T(8,128)(2,1)S(1)}, bf16[1,128,768]{2,1,0:T(8,128)(2,1)}, u32[]{:S(2)}) copy-start(bf16[1,128,768]{2,1,0:T(8,128)(2,1)} %param.23) | copy-start | bytes 589828
  0.7 9.1 %copy-start.70 = (f32[768]{0:T(1024)S(1)}, f32[768]{0:T(1024)}, u32[]{:S(2)}) copy-start(f32[768]{0:T(1024)} %param.31) | copy-start | bytes 9220
  0.7 10.3 %copy-start.85 = (f32[768]{0:T(1024)S(1)}, f32[768]{0:T(1024)}, u32[]{:S(2)}) copy-start(f32[768]{0:T(1024)} %param.30) | copy-start | bytes 9220
  0.7 10.9 %copy-start.49 = (f32[768]{0:T(1024)S(1)}, f32[768]{0:T(1024)}, u32[]{:S(2)}) copy-start(f32[768]{0:T(1024)} %param.27) | copy-start | bytes 9220
  0.7 10.9 %copy-start.65 = (f32[768]{0:T(1024)S(1)}, f32[768]{0:T(1024)}, u32[]{:S(2)}) copy-start(f32[768]{0:T(1024)} %param.28) | copy-start | bytes 9220
  3.0 27.8 %all-to-all-start = ((bf16[8,128,768]{2,1,0:T(8,128)(2,1)}), bf16[8,128,768]{2,1,0:T(8,128)(2,1)S(1)}, u32[]{:S(2)}, u32[]{:S(2)}) async-start(bf16[8,128,768]{2,1,0:T(8,128)(2,1)} %broadcast_in_dim.42), calls=%async_computation | async-start | bytes 3145728 | tf_op jit(solution)/shard_map/all_to_all | solution.py:54
  8.6 11.5 %copy-start.33 = (bf16[1,128,768]{2,1,0:T(8,128)(2,1)S(1)}, bf16[1,128,768]{2,1,0:T(8,128)(2,1)}, u32[]{:S(2)}) copy-start(bf16[1,128,768]{2,1,0:T(8,128)(2,1)} %param.24) | copy-start | bytes 589828
  17.0 13.8 %copy-start.56 = (f32[128]{0:T(128)}, f32[128]{0:T(128)S(1)}, u32[]{:S(2)}) copy-start(f32[128]{0:T(128)S(1)} %get-tuple-element.187) | copy-start | bytes 1540
  19.3 12.8 %copy-start.50 = (f32[768]{0:T(1024)S(1)}, f32[768]{0:T(1024)}, u32[]{:S(2)}) copy-start(f32[768]{0:T(1024)} %param.27) | copy-start | bytes 9220
  19.3 12.8 %copy-start.66 = (f32[768]{0:T(1024)S(1)}, f32[768]{0:T(1024)}, u32[]{:S(2)}) copy-start(f32[768]{0:T(1024)} %param.28) | copy-start | bytes 9220
  50.2 6.9 %slice-start.2 = ((s8[4718592]{0:T(1024)(128)(4,1)}), s8[4194304]{0:T(1024)(128)(4,1)S(1)}, s32[]{:S(2)}) async-start(s8[4718592]{0:T(1024)(128)(4,1)} %bitcast.240), calls=%async_computation.13 | async-start | bytes 8388608
  50.2 5.4 %copy-start.53 = (f32[128]{0:T(128)S(1)}, f32[128]{0:T(128)}, u32[]{:S(2)}) copy-start(f32[128]{0:T(128)} %copy-done.52) | copy-start | bytes 1540
  50.2 5.4 %copy-start.62 = (f32[128]{0:T(128)S(1)}, f32[128]{0:T(128)}, u32[]{:S(2)}) copy-start(f32[128]{0:T(128)} %get-tuple-element.186) | copy-start | bytes 1540
  50.2 5.4 %copy-start.67 = (f32[768]{0:T(1024)S(1)}, f32[768]{0:T(1024)}, u32[]{:S(2)}) copy-start(f32[768]{0:T(1024)} %param.33) | copy-start | bytes 9220
  50.2 6.9 %slice-start.3 = ((s8[4718592]{0:T(1024)(128)(4,1)}), s8[524288]{0:T(1024)(128)(4,1)S(1)}, s32[]{:S(2)}) async-start(s8[4718592]{0:T(1024)(128)(4,1)} %bitcast.240), calls=%async_computation.14 | async-start | bytes 1048576
  67.8 5.4 %copy-start.3 = (bf16[1024,768]{1,0:T(8,128)(2,1)S(1)}, bf16[1024,768]{1,0:T(8,128)(2,1)}, u32[]{:S(2)}) copy-start(bf16[1024,768]{1,0:T(8,128)(2,1)} %copy-done.2) | copy-start | bytes 4718596
  77.6 18.6 %copy-start.82 = (f32[128]{0:T(128)S(1)}, f32[128]{0:T(128)}, u32[]{:S(2)}) copy-start(f32[128]{0:T(128)} %dynamic_slice.164) | copy-start | bytes 1540
  88.8 18.5 %all-to-all-start.1 = ((bf16[8,128,256]{2,1,0:T(8,128)(2,1)}), bf16[8,128,256]{2,1,0:T(8,128)(2,1)}, u32[]{:S(2)}, u32[]{:S(2)}) async-start(bf16[8,128,256]{2,1,0:T(8,128)(2,1)} %fusion.95), calls=%async_computation.1 | async-start | bytes 1048576 | tf_op jit(solution)/shard_map/all_to_all | solution.py:221
  98.6 8.7 %copy-start.32 = (bf16[128,768]{1,0:T(8,128)(2,1)S(1)}, bf16[128,768]{1,0:T(8,128)(2,1)}, u32[]{:S(2)}) copy-start(bf16[128,768]{1,0:T(8,128)(2,1)} %copy.123) | copy-start | bytes 589828
  108.5 8.7 %copy-start.55 = (f32[2,1024]{1,0:T(2,128)S(1)}, f32[2,1024]{1,0:T(2,128)}, u32[]{:S(2)}) copy-start(f32[2,1024]{1,0:T(2,128)} %get-tuple-element.177) | copy-start | bytes 24580
  108.5 32.5 %all-to-all-start.3 = ((bf16[8,128,768]{2,1,0:T(8,128)(2,1)}), bf16[8,128,768]{2,1,0:T(8,128)(2,1)}, u32[]{:S(2)}, u32[]{:S(2)}) async-start(bf16[8,128,768]{2,1,0:T(8,128)(2,1)} %broadcast_in_dim.49), calls=%async_computation.3 | async-start | bytes 3145728 | tf_op jit(solution)/shard_map/all_to_all | solution.py:54
  117.2 4.9 %copy-start.36 = (bf16[1024,128]{0,1:T(8,128)(2,1)S(1)}, bf16[1024,128]{0,1:T(8,128)(2,1)}, u32[]{:S(2)}) copy-start(bf16[1024,128]{0,1:T(8,128)(2,1)} %fusion.27) | copy-start | bytes 786436
  117.2 4.9 %copy-start.37 = (bf16[1024,128]{0,1:T(8,128)(2,1)S(1)}, bf16[1024,128]{0,1:T(8,128)(2,1)}, u32[]{:S(2)}) copy-start(bf16[1024,128]{0,1:T(8,128)(2,1)} %copy.117) | copy-start | bytes 786436
  122.1 4.9 %slice-start = ((s8[8388608]{0:T(1024)(128)(4,1)}), s8[4194304]{0:T(1024)(128)(4,1)S(1)}, s32[]{:S(2)}) async-start(s8[8388608]{0:T(1024)(128)(4,1)} %bitcast.233), calls=%async_computation.11 | async-start | bytes 8388608
  122.2 5.8 %slice-start.1 = ((s8[8388608]{0:T(1024)(128)(4,1)}), s8[4194304]{0:T(1024)(128)(4,1)S(1)}, s32[]{:S(2)}) async-start(s8[8388608]{0:T(1024)(128)(4,1)} %bitcast.233), calls=%async_computation.12 | async-start | bytes 8388608
  141.0 6.8 %copy-start.60 = (f32[1,1024]{1,0:T(1,128)S(1)}, f32[1,1024]{1,0:T(1,128)}, u32[]{:S(2)}) copy-start(f32[1,1024]{1,0:T(1,128)} %copy-done.59) | copy-start | bytes 12292
  142.3 5.6 %copy-start.68 = (f32[768]{0:T(1024)S(1)}, f32[768]{0:T(1024)}, u32[]{:S(2)}) copy-start(f32[768]{0:T(1024)} %param.33) | copy-start | bytes 9220
  142.3 26.5 %all-to-all-start.4 = ((bf16[8,128,768]{2,1,0:T(8,128)(2,1)}), bf16[8,128,768]{2,1,0:T(8,128)(2,1)}, u32[]{:S(2)}, u32[]{:S(2)}) async-start(bf16[8,128,768]{2,1,0:T(8,128)(2,1)} %broadcast_in_dim.51), calls=%async_computation.4 | async-start | bytes 3145728 | tf_op jit(solution)/shard_map/all_to_all | solution.py:54
  168.8 19.6 %all-to-all-start.2 = ((bf16[8,128,288]{1,2,0:T(8,128)(2,1)}), bf16[8,128,288]{1,2,0:T(8,128)(2,1)}, u32[]{:S(2)}, u32[]{:S(2)}) async-start(bf16[8,128,288]{1,2,0:T(8,128)(2,1)} %copy_bitcast_fusion), calls=%async_computation.2 | async-start | bytes 1179648 | tf_op jit(solution)/shard_map/all_to_all | solution.py:257
  173.0 4.4 copy-start.87
  182.0 25.9 %collective-permute-start = (bf16[400,384]{1,0:T(8,128)(2,1)}, bf16[400,384]{1,0:T(8,128)(2,1)}, u32[]{:S(2)}, u32[]{:S(2)}) collective-permute-start(bf16[400,384]{1,0:T(8,128)(2,1)} %pad_maximum_fusion.13), channel_id=1, source_target_pairs={{0,8},{8,0},{1,9},{9,1},{2,10},{10,2},{3,11},{11,3},{4,12},{12,4},... | collective-permute-start | bytes 921608 | tf_op jit(solution)/shard_map/ppermute | solution.py:78
  185.5 2.1 collective-permute-start.4
  187.3 9.6 %collective-permute-start.8 = (bf16[384,384]{1,0:T(8,128)(2,1)}, bf16[384,384]{1,0:T(8,128)(2,1)}, u32[]{:S(2)}, u32[]{:S(2)}) collective-permute-start(bf16[384,384]{1,0:T(8,128)(2,1)} %fusion.69), channel_id=1, source_target_pairs={{0,8},{8,0},{1,9},{9,1},{2,10},{10,2},{3,11},{11,3},{4,12},{12,4},... | collective-permute-start | bytes 884744 | tf_op jit(solution)/shard_map/ppermute | solution.py:78
  188.4 12.9 %all-to-all-start.7 = ((bf16[8,48,384]{2,1,0:T(8,128)(2,1)}), bf16[8,48,384]{2,1,0:T(8,128)(2,1)S(1)}, u32[]{:S(2)}, u32[]{:S(2)}) async-start(bf16[8,48,384]{2,1,0:T(8,128)(2,1)} %bitcast.255), calls=%async_computation.7 | async-start | bytes 589824 | tf_op jit(solution)/shard_map/all_to_all | solution.py:95
  201.2 11.8 %all-to-all-start.9 = ((bf16[8,48,384]{2,1,0:T(8,128)(2,1)}), bf16[8,48,384]{2,1,0:T(8,128)(2,1)S(1)}, u32[]{:S(2)}, u32[]{:S(2)}) async-start(bf16[8,48,384]{2,1,0:T(8,128)(2,1)} %bitcast.77), calls=%async_computation.9 | async-start | bytes 589824 | tf_op jit(solution)/shard_map/all_to_all | solution.py:95
  213.0 11.9 %all-to-all-start.5 = ((bf16[8,64,384]{2,1,0:T(8,128)(2,1)}), bf16[8,64,384]{2,1,0:T(8,128)(2,1)S(1)}, u32[]{:S(2)}, u32[]{:S(2)}) async-start(bf16[8,64,384]{2,1,0:T(8,128)(2,1)} %pad_maximum_fusion.12), calls=%async_computation.5 | async-start | bytes 786432 | tf_op jit(solution)/shard_map/all_to_all | solution.py:95
  225.8 12.9 %all-to-all-start.8 = ((bf16[16,48,384]{2,1,0:T(8,128)(2,1)}), bf16[16,48,384]{2,1,0:T(8,128)(2,1)S(1)}, u32[]{:S(2)}, u32[]{:S(2)}) async-start(bf16[16,48,384]{2,1,0:T(8,128)(2,1)} %broadcast_in_dim.55), calls=%async_computation.8 | async-start | bytes 1179648 | tf_op jit(solution)/shard_map/all_to_all | solution.py:54
  231.6 30.0 %copy-start.83 = (s32[4]{0:T(128)S(1)}, s32[4]{0:T(128)}, u32[]{:S(2)}) copy-start(s32[4]{0:T(128)} %constant.203.clone) | copy-start | bytes 52
  231.6 30.0 %copy-start.84 = (s32[4]{0:T(128)S(1)}, s32[4]{0:T(128)}, u32[]{:S(2)}) copy-start(s32[4]{0:T(128)} %constant.204.clone) | copy-start | bytes 52
  239.6 14.7 %all-to-all-start.10 = ((bf16[16,48,384]{2,1,0:T(8,128)(2,1)}), bf16[16,48,384]{2,1,0:T(8,128)(2,1)S(1)}, u32[]{:S(2)}, u32[]{:S(2)}) async-start(bf16[16,48,384]{2,1,0:T(8,128)(2,1)} %broadcast_in_dim.56), calls=%async_computation.10 | async-start | bytes 1179648 | tf_op jit(solution)/shard_map/all_to_all | solution.py:54
  244.9 41.0 %collective-permute-start.5 = (bf16[16,48,384]{2,1,0:T(8,128)(2,1)S(1)}, bf16[16,48,384]{2,1,0:T(8,128)(2,1)}, u32[]{:S(2)}, u32[]{:S(2)}) collective-permute-start(bf16[16,48,384]{2,1,0:T(8,128)(2,1)S(1)} %all-to-all-done.8), channel_id=1, source_target_pairs={{0,2},{2,0},{4,6},{6,4},{8,14},{10,12},{12,10},{14,8},{1,3},{3,1},... | collective-permute-start | bytes 1769480 | tf_op jit(solution)/shard_map/ppermute | solution.py:74
  247.6 42.2 %copy-start.9 = (f32[128,3072]{1,0:T(8,128)S(1)}, f32[128,3072]{1,0:T(8,128)}, u32[]{:S(2)}) copy-start(f32[128,3072]{1,0:T(8,128)} %convolution_add_fusion) | copy-start | bytes 4718596
  247.6 42.2 %copy-start.57 = (f32[128]{0:T(128)S(1)}, f32[128]{0:T(128)}, u32[]{:S(2)}) copy-start(f32[128]{0:T(128)} %copy-done.56) | copy-start | bytes 1540
  247.6 42.2 %copy-start.69 = (f32[768]{0:T(1024)S(1)}, f32[768]{0:T(1024)}, u32[]{:S(2)}) copy-start(f32[768]{0:T(1024)} %param.39) | copy-start | bytes 9220
  254.4 42.5 %copy-start.22 = (bf16[16,48,384]{2,1,0:T(8,128)(2,1)}, bf16[16,48,384]{2,1,0:T(8,128)(2,1)S(1)}, u32[]{:S(2)}) copy-start(bf16[16,48,384]{2,1,0:T(8,128)(2,1)S(1)} %all-to-all-done.10) | copy-start | bytes 1769476
  255.4 39.4 %all-to-all-start.6 = ((bf16[16,64,384]{2,1,0:T(8,128)(2,1)}), bf16[16,64,384]{2,1,0:T(8,128)(2,1)}, u32[]{:S(2)}, u32[]{:S(2)}) async-start(bf16[16,64,384]{2,1,0:T(8,128)(2,1)} %broadcast_in_dim.54), calls=%async_computation.6 | async-start | bytes 1572864 | tf_op jit(solution)/shard_map/all_to_all | solution.py:54
  285.6 11.3 %collective-permute-start.9 = (bf16[16,48,384]{2,1,0:T(8,128)(2,1)S(1)}, bf16[16,48,384]{2,1,0:T(8,128)(2,1)}, u32[]{:S(2)}, u32[]{:S(2)}) collective-permute-start(bf16[16,48,384]{2,1,0:T(8,128)(2,1)S(1)} %all-to-all-done.10), channel_id=1, source_target_pairs={{0,1},{1,0},{8,73},{9,72},{64,65},{65,64},{72,9},{73,8},{2,3},{3,2... | collective-permute-start | bytes 1769480 | tf_op jit(solution)/shard_map/ppermute | solution.py:74
  288.1 18.7 %collective-permute-start.6 = (bf16[2,16,48,384]{3,2,1,0:T(8,128)(2,1)}, bf16[2,16,48,384]{3,2,1,0:T(8,128)(2,1)}, u32[]{:S(2)}, u32[]{:S(2)}) collective-permute-start(bf16[2,16,48,384]{3,2,1,0:T(8,128)(2,1)} %pad_maximum_fusion.8), channel_id=1, source_target_pairs={{0,6},{2,4},{4,2},{6,0},{8,10},{10,8},{12,14},{14,12},{1,7},{3,5},... | collective-permute-start | bytes 3538952 | tf_op jit(solution)/shard_map/ppermute | solution.py:74
  296.2 10.4 %collective-permute-start.1 = (bf16[16,48,384]{2,1,0:T(8,128)(2,1)S(1)}, bf16[16,48,384]{2,1,0:T(8,128)(2,1)S(1)}, u32[]{:S(2)}, u32[]{:S(2)}) collective-permute-start(bf16[16,48,384]{2,1,0:T(8,128)(2,1)S(1)} %get-tuple-element.126), channel_id=1, source_target_pairs={{0,16},{8,56},{16,0},{24,40},{32,48},{40,24},{48,32},{56,8},{1,17}... | collective-permute-start | bytes 1769480 | tf_op jit(solution)/shard_map/ppermute | solution.py:74
  298.0 28.8 %collective-permute-start.10 = (bf16[2,16,48,384]{3,2,1,0:T(8,128)(2,1)S(1)}, bf16[2,16,48,384]{3,2,1,0:T(8,128)(2,1)S(1)}, u32[]{:S(2)}, u32[]{:S(2)}) collective-permute-start(bf16[2,16,48,384]{3,2,1,0:T(8,128)(2,1)S(1)} %pad_maximum_fusion.10), channel_id=1, source_target_pairs={{0,65},{1,64},{8,9},{9,8},{64,1},{65,0},{72,73},{73,72},{2,67},{3,... | collective-permute-start | bytes 3538952 | tf_op jit(solution)/shard_map/ppermute | solution.py:74
  306.8 24.6 %collective-permute-start.2 = (bf16[2,16,48,384]{3,2,1,0:T(8,128)(2,1)S(1)}, bf16[2,16,48,384]{3,2,1,0:T(8,128)(2,1)S(1)}, u32[]{:S(2)}, u32[]{:S(2)}) collective-permute-start(bf16[2,16,48,384]{3,2,1,0:T(8,128)(2,1)S(1)} %pad_maximum_fusion.7), channel_id=1, source_target_pairs={{0,48},{8,24},{16,32},{24,8},{32,16},{40,56},{48,0},{56,40},{1,49}... | collective-permute-start | bytes 3538952 | tf_op jit(solution)/shard_map/ppermute | solution.py:74
  308.8 18.0 %copy-start.23 = (bf16[16,48,384]{2,1,0:T(8,128)(2,1)S(1)}, bf16[16,48,384]{2,1,0:T(8,128)(2,1)}, u32[]{:S(2)}) copy-start(bf16[16,48,384]{2,1,0:T(8,128)(2,1)} %copy-done.22) | copy-start | bytes 1769476
  310.6 37.7 %collective-permute-start.7 = (bf16[4,16,48,384]{3,2,1,0:T(8,128)(2,1)}, bf16[4,16,48,384]{3,2,1,0:T(8,128)(2,1)}, u32[]{:S(2)}, u32[]{:S(2)}) collective-permute-start(bf16[4,16,48,384]{3,2,1,0:T(8,128)(2,1)} %pad_maximum_fusion.3), channel_id=1, source_target_pairs={{0,8},{8,0},{1,9},{9,1},{2,10},{10,2},{3,11},{11,3},{4,12},{12,4},... | collective-permute-start | bytes 7077896 | tf_op jit(solution)/shard_map/ppermute | solution.py:78
  330.5 39.5 %collective-permute-start.11 = (bf16[4,16,48,384]{3,2,1,0:T(8,128)(2,1)}, bf16[4,16,48,384]{3,2,1,0:T(8,128)(2,1)}, u32[]{:S(2)}, u32[]{:S(2)}) collective-permute-start(bf16[4,16,48,384]{3,2,1,0:T(8,128)(2,1)} %pad_maximum_fusion.5), channel_id=1, source_target_pairs={{0,8},{8,0},{1,9},{9,1},{2,10},{10,2},{3,11},{11,3},{4,12},{12,4},... | collective-permute-start | bytes 7077896 | tf_op jit(solution)/shard_map/ppermute | solution.py:78
  333.9 55.6 %collective-permute-start.3 = (bf16[4,16,48,384]{3,2,1,0:T(8,128)(2,1)}, bf16[4,16,48,384]{3,2,1,0:T(8,128)(2,1)}, u32[]{:S(2)}, u32[]{:S(2)}) collective-permute-start(bf16[4,16,48,384]{3,2,1,0:T(8,128)(2,1)} %pad_maximum_fusion.1), channel_id=1, source_target_pairs={{0,8},{8,0},{1,9},{9,1},{2,10},{10,2},{3,11},{11,3},{4,12},{12,4},... | collective-permute-start | bytes 7077896 | tf_op jit(solution)/shard_map/ppermute | solution.py:78
  357.0 13.0 %copy-start.11 = (bf16[1,16,48,384]{3,2,1,0:T(8,128)(2,1)S(1)}, bf16[1,16,48,384]{3,2,1,0:T(8,128)(2,1)}, u32[]{:S(2)}) copy-start(bf16[1,16,48,384]{3,2,1,0:T(8,128)(2,1)} %copy-done.10) | copy-start | bytes 1769476
  357.0 13.0 %copy-start.13 = (bf16[1,16,48,384]{3,2,1,0:T(8,128)(2,1)S(1)}, bf16[1,16,48,384]{3,2,1,0:T(8,128)(2,1)}, u32[]{:S(2)}) copy-start(bf16[1,16,48,384]{3,2,1,0:T(8,128)(2,1)} %copy-done.12) | copy-start | bytes 1769476
  357.0 13.0 %copy-start.15 = (bf16[1,16,48,384]{3,2,1,0:T(8,128)(2,1)S(1)}, bf16[1,16,48,384]{3,2,1,0:T(8,128)(2,1)}, u32[]{:S(2)}) copy-start(bf16[1,16,48,384]{3,2,1,0:T(8,128)(2,1)} %copy-done.14) | copy-start | bytes 1769476
  385.1 4.4 copy-start.17
  385.1 4.4 copy-start.19
  385.1 4.4 copy-start.21
  441.3 10.0 %copy-start.1 = (bf16[768,768]{1,0:T(8,128)(2,1)S(1)}, bf16[768,768]{1,0:T(8,128)(2,1)}, u32[]{:S(2)}) copy-start(bf16[768,768]{1,0:T(8,128)(2,1)} %param.32) | copy-start | bytes 3538948
  (52 other events, 127.5 us)

commit v2 on v1

v2 whole, which is shorter than its diff:
```python
import math

import jax
import jax.numpy as jnp
from jax import lax
from jax.experimental import pallas as pl
from jax.experimental.pallas import tpu as pltpu
from jax.sharding import Mesh
from jax.sharding import PartitionSpec as P

D = 768
HEADS = 12
HEAD_DIM = 64
FF = 3072
IMGS = 4
TP = 8
COLS = D // TP
HID = FF // TP
PAIR = 2 * HEAD_DIM
VEC_ROWS = 16
PIECE = (2 * TP, HID // TP, HID)

eps_norm = 1e-06
drop_scale = 1.0 / 0.9
far_below = -1e30
inv_root_two = 1.0 / math.sqrt(2.0)
inv_root_tau = 1.0 / math.sqrt(2.0 * math.pi)

BLK = ("x", "yl")
bf16 = jnp.bfloat16
f32 = jnp.float32


def dot(a, b, dims):
    return lax.dot_general(a, b, ((dims[0], dims[1]), ((), ())), preferred_element_type=f32)


def normalize(values):
    mean = jnp.mean(values, axis=-1, keepdims=True)
    centred = values - mean
    inverse = lax.rsqrt(jnp.mean(centred * centred, axis=-1, keepdims=True) + eps_norm)
    return (centred * inverse, inverse)


def norm_back(grad_out, normed, inverse, gain):
    scaled = grad_out * gain
    inner = (
        scaled
        - jnp.mean(scaled, axis=-1, keepdims=True)
        - normed * jnp.mean(scaled * normed, axis=-1, keepdims=True)
    )
    return (inverse * inner, jnp.sum(grad_out * normed, axis=0), jnp.sum(grad_out, axis=0))


def spread(block, axes, count):
    tiled = jnp.broadcast_to(block[None], (count,) + block.shape)
    return lax.all_to_all(tiled, axes, 0, 0)


def exchange(block, axis, by_core):
    sizes = [2 if name in ("c", "yh", "yl") else 4 for name in axis]
    route = []
    for place in range(math.prod(sizes)):
        left, spots = place, {}
        for name, size in reversed(list(zip(axis, sizes))):
            left, spots[name] = divmod(left, size)
        mask = by_core[spots["c"]]
        if "yh" in spots:
            spots["yh"] ^= mask // 2
            spots["yl"] ^= mask % 2
        else:
            spots[axis[0] if axis[0] != "c" else axis[1]] ^= mask
        partner = 0
        for name, size in zip(axis, sizes):
            partner = partner * size + spots[name]
        route.append((place, partner))
    return lax.ppermute(block, axis, route)


def swap_core(block):
    return lax.ppermute(block, "c", [(0, 1), (1, 0)])


def sum_rows(partial, extra):
    core = lax.axis_index("c")
    halves = partial.reshape(2, HID, HID)
    mine = lax.dynamic_index_in_dim(halves, core, 0, keepdims=False)
    other = lax.dynamic_index_in_dim(halves, 1 - core, 0, keepdims=False)
    if extra is not None:
        mine = jnp.concatenate([mine, extra], axis=0)
        other = jnp.concatenate([other, extra], axis=0)
    got = swap_core(other.astype(bf16))
    half = (mine + got.astype(f32)).astype(bf16)
    pieces = half[:HID].reshape(8, HID // 8, HID)
    if extra is not None:
        tail = jnp.broadcast_to(half[HID:][None], (8, VEC_ROWS, HID))
        pieces = jnp.concatenate([pieces, tail], axis=1)
    pieces = lax.all_to_all(pieces, ("yh", "z"), 0, 0)
    return jnp.sum(pieces.astype(f32), axis=0).astype(bf16)


def whole(shape):
    return pl.BlockSpec(shape, lambda *_: (0,) * len(shape))


def column(v):
    return v.reshape(-1, 1)


def line(v):
    return v.reshape(1, -1)


def gelu_parts(u):
    cumulative = 0.5 * (1.0 + lax.erf(u * inv_root_two))
    density = jnp.exp(-0.5 * u * u) * inv_root_tau
    return (u * cumulative, cumulative + u * density)


def launch(body, grid, scalars, ins, outs, scratch, flops, moved):
    arrays = [a for a, _ in ins]
    return pl.pallas_call(
        body,
        grid_spec=pltpu.PrefetchScalarGridSpec(
            num_scalar_prefetch=1,
            grid=grid,
            in_specs=[spec for _, spec in ins],
            out_specs=[spec for _, spec in outs],
            scratch_shapes=scratch,
        ),
        out_shape=[shape for shape, _ in outs],
        compiler_params=pltpu.CompilerParams(vmem_limit_bytes=56 * 1024 * 1024),
        cost_estimate=pl.CostEstimate(flops=flops, bytes_accessed=moved, transcendentals=0),
    )(scalars, *arrays)


def shaped(shape, dtype):
    return jax.ShapeDtypeStruct(shape, dtype)


def attend_kernel(
    at, x, ids_col, ids_row, gain, bias, wq, wk, wv, bq, bv, out, h_all, xhat_all, block
):
    row = x.shape[0]
    tokens = out.shape[0]
    here = pl.multiple_of(at[0], tokens)

    @pl.when(pl.program_id(0) == 0)
    def _():
        def norm(i, _):
            spot = pl.ds(pl.multiple_of(i * tokens, tokens), tokens)
            valid = (ids_col[spot] < IMGS).astype(f32)
            normed, _inverse = normalize(x[spot].astype(f32) * valid)
            xhat_all[spot] = normed.astype(bf16)
            h_all[spot] = (normed * gain[...] + bias[...]).astype(bf16)
            return 0

        lax.fori_loop(0, row // tokens, norm, 0)
        mine = ids_col[pl.ds(here, tokens)]
        block[...] = jnp.where(mine == ids_row[...], 0.0, far_below)

    h = h_all[...]
    keys = dot(h, wk[...], ((1,), (0,))).astype(bf16)
    values = (dot(h, wv[...], ((1,), (0,))) + bv[...]).astype(bf16)
    query = dot(h_all[pl.ds(here, tokens)], wq[...], ((1,), (0,))) + bq[...]
    low = lax.broadcasted_iota(jnp.int32, (tokens, PAIR), 1) < HEAD_DIM
    both = jnp.concatenate([jnp.where(low, query, 0.0), jnp.where(low, 0.0, query)])
    scores = dot(both.astype(bf16), keys, ((1,), (1,))) * HEAD_DIM**-0.5
    scores = scores.reshape(2, tokens, row) + block[...][None]
    scores = scores.reshape(2 * tokens, row)
    expo = jnp.exp(scores - jnp.max(scores, axis=-1, keepdims=True))
    probs = (expo * (1.0 / jnp.sum(expo, axis=-1, keepdims=True))).astype(bf16)
    result = dot(probs, values, ((1,), (0,)))
    out[...] = jnp.where(low, result[:tokens], result[tokens:]).astype(bf16)


def attend(at, x_all, ids, gain, bias, w_qkv, b_query, b_value, tokens):
    row, width = x_all.shape
    steps = width // PAIR
    part = pl.BlockSpec((width, PAIR), lambda p, _: (0, p))
    part_k = pl.BlockSpec((width, PAIR), lambda p, _: (0, steps + p))
    part_v = pl.BlockSpec((width, PAIR), lambda p, _: (0, 2 * steps + p))
    small = pl.BlockSpec((1, PAIR), lambda p, _: (0, p))
    return launch(
        attend_kernel,
        (steps,),
        at,
        [
            (x_all, whole((row, width))),
            (column(ids), whole((row, 1))),
            (line(ids), whole((1, row))),
            (line(gain), whole((1, width))),
            (line(bias), whole((1, width))),
            (w_qkv, part),
            (w_qkv, part_k),
            (w_qkv, part_v),
            (line(b_query), small),
            (line(b_value), small),
        ],
        [
            (shaped((tokens, width), bf16), pl.BlockSpec((tokens, PAIR), lambda p, _: (0, p))),
            (shaped((row, width), bf16), whole((row, width))),
            (shaped((row, width), bf16), whole((row, width))),
        ],
        [pltpu.VMEM((tokens, row), f32)],
        6 * 10**9,
        10**7,
    )


def first_head(j):
    return 3 * (j // 2) + j % 2


def mlp_kernel(
    _,
    att,
    x,
    marks,
    grad_z,
    w_proj,
    b_proj,
    gain,
    bias,
    w_one,
    b_one,
    w_two,
    b_two,
    out,
    grad_mid,
    outgoing,
    sums,
    mid,
    normed,
    inverse,
    h_two,
    grad_mlp,
    total,
    grad_h,
):
    step = pl.program_id(0)
    scale_attn, scale_mlp = marks[:, 0:1], marks[:, 1:2]

    @pl.when(step == 0)
    def _():
        branch = dot(att[...], w_proj[...], ((1,), (0,))) + b_proj[...]
        y = x[...].astype(f32) * marks[:, 2:3] + scale_attn * branch
        mid[...] = y
        hat, inv = normalize(y)
        normed[...] = hat
        inverse[...] = inv
        h_two[...] = (hat * gain[...] + bias[...]).astype(bf16)
        grad_mlp[...] = (scale_mlp * grad_z[...].astype(f32)).astype(bf16)
        total[...] = jnp.zeros_like(total)
        grad_h[...] = jnp.zeros_like(grad_h)

    hidden = dot(h_two[...], w_one[...], ((1,), (0,))) + b_one[...]
    gelled, slope = gelu_parts(hidden)
    total[...] += dot(gelled.astype(bf16), w_two[...], ((1,), (0,)))
    grad_hidden = (dot(grad_mlp[...], w_two[...], ((1,), (1,))) * slope).astype(bf16)
    grad_h[...] += dot(grad_hidden, w_one[...], ((1,), (1,)))

    @pl.when(step == pl.num_programs(0) - 1)
    def _():
        out[...] = (mid[...] + scale_mlp * (total[...] + b_two[...])).astype(bf16)
        back, gain_sum, bias_sum = norm_back(grad_h[...], normed[...], inverse[...], gain[...])
        grad_y = grad_z[...].astype(f32) + back
        grad_mid[...] = grad_y
        sums[0:1] = line(gain_sum)
        sums[1:2] = line(bias_sum)
        sums[2:3] = line(jnp.sum(grad_mlp[...].astype(f32), axis=0))
        sums[3:8] = jnp.zeros((5, sums.shape[1]), f32)
        branch_t = jnp.transpose(scale_attn * grad_y).astype(bf16)
        att_t = dot(w_proj[...], branch_t, ((1,), (0,))).astype(bf16)
        for j in range(TP):
            start = first_head(j) * HEAD_DIM
            outgoing[j, :PAIR] = att_t[start : start + PAIR]
            outgoing[j, PAIR:] = branch_t[j * COLS : (j + 1) * COLS]


def mlp(att, x, marks, grad_z, w_proj, b_proj, gain, bias, w_one, b_one, w_two, b_two):
    tokens, width = x.shape
    chunk = 512
    tw = whole((tokens, width))
    return launch(
        mlp_kernel,
        (FF // chunk,),
        jnp.zeros((1,), jnp.int32),
        [
            (att, tw),
            (x, tw),
            (marks, whole(marks.shape)),
            (grad_z, tw),
            (w_proj, whole((width, width))),
            (line(b_proj), whole((1, width))),
            (line(gain), whole((1, width))),
            (line(bias), whole((1, width))),
            (w_one, pl.BlockSpec((width, chunk), lambda p, _: (0, p))),
            (line(b_one), pl.BlockSpec((1, chunk), lambda p, _: (0, p))),
            (w_two, pl.BlockSpec((chunk, width), lambda p, _: (p, 0))),
            (line(b_two), whole((1, width))),
        ],
        [
            (shaped((tokens, width), bf16), tw),
            (shaped((tokens, width), f32), tw),
            (shaped((TP, PAIR + COLS, tokens), bf16), whole((TP, PAIR + COLS, tokens))),
            (shaped((8, width), f32), whole((8, width))),
        ],
        [
            pltpu.VMEM((tokens, width), f32),
            pltpu.VMEM((tokens, width), f32),
            pltpu.VMEM((tokens, 1), f32),
            pltpu.VMEM((tokens, width), bf16),
            pltpu.VMEM((tokens, width), bf16),
            pltpu.VMEM((tokens, width), f32),
            pltpu.VMEM((tokens, width), f32),
        ],
        3 * 10**9,
        11 * 10**6,
    )


def pair_kernel(_, h, w, b, ids_col, ids_row, query, key_t, value, probs, att_t, keys, value_t):
    block = probs.shape[2]

    @pl.when(pl.program_id(0) == 0)
    def _():
        def make(i, _):
            spot = pl.ds(pl.multiple_of(i * block, block), block)
            qkv = dot(h[spot], w[...], ((1,), (0,))) + b[...]
            query[spot] = qkv[:, :PAIR].astype(bf16)
            keys[spot] = qkv[:, PAIR : 2 * PAIR].astype(bf16)
            value[spot] = qkv[:, 2 * PAIR :].astype(bf16)
            key_t[:, spot] = jnp.transpose(qkv[:, PAIR : 2 * PAIR]).astype(bf16)
            value_t[:, spot] = jnp.transpose(qkv[:, 2 * PAIR :]).astype(bf16)
            return 0

        lax.fori_loop(0, h.shape[0] // block, make, 0)

    here = pl.ds(pl.multiple_of(pl.program_id(0) * block, block), block)
    allowed = ids_col[...] == ids_row[...]
    k = keys[...]
    low = lax.broadcasted_iota(jnp.int32, k.shape, 1) < HEAD_DIM
    for e in range(2):
        k_e = jnp.where(low == (e == 0), k, jnp.zeros_like(k))
        scores = dot(k_e, query[here], ((1,), (1,))) * HEAD_DIM**-0.5
        scores = jnp.where(allowed, scores, far_below)
        expo = jnp.exp(scores - jnp.max(scores, axis=0, keepdims=True))
        p = (expo * (1.0 / jnp.sum(expo, axis=0, keepdims=True))).astype(bf16)
        probs[e] = p
        rows = slice(e * HEAD_DIM, (e + 1) * HEAD_DIM)
        att_t[rows] = dot(value_t[rows], p, ((1,), (0,)))


def pair_forward(h_all, w, b, ids):
    row, width = h_all.shape
    block = 256
    return launch(
        pair_kernel,
        (row // block,),
        jnp.zeros((1,), jnp.int32),
        [
            (h_all, whole((row, width))),
            (w, whole(w.shape)),
            (line(b), whole((1, 3 * PAIR))),
            (column(ids), whole((row, 1))),
            (line(ids), pl.BlockSpec((1, block), lambda i, _: (0, i))),
        ],
        [
            (shaped((row, PAIR), bf16), whole((row, PAIR))),
            (shaped((PAIR, row), bf16), whole((PAIR, row))),
            (shaped((row, PAIR), bf16), whole((row, PAIR))),
            (shaped((2, row, row), bf16), pl.BlockSpec((2, row, block), lambda i, _: (0, 0, i))),
            (shaped((PAIR, row), f32), pl.BlockSpec((PAIR, block), lambda i, _: (0, i))),
        ],
        [pltpu.VMEM((row, PAIR), bf16), pltpu.VMEM((PAIR, row), bf16)],
        3 * 10**9,
        8 * 10**6,
    )


def pair_back_kernel(
    shift,
    incoming,
    query,
    key_t,
    value,
    probs,
    att_t,
    h,
    xhat,
    w_t,
    grad_b,
    outgoing,
    sums,
    col_sums,
    grad_t,
    grad_rows,
    delta,
    d_t,
    d_key,
    d_value,
    flat,
):
    step = pl.program_id(0)
    tokens = incoming.shape[2]
    block = value.shape[0]

    @pl.when(step == 0)
    def _():
        for t in range(TP):
            spot = slice(t * tokens, (t + 1) * tokens)
            piece = incoming[t, :PAIR]
            grad_t[:, spot] = piece
            grad_rows[spot] = jnp.transpose(piece.astype(f32)).astype(bf16)
        prod = grad_t[...].astype(f32) * att_t[...]
        delta[0:1] = jnp.sum(prod[:HEAD_DIM], axis=0, keepdims=True)
        delta[1:2] = jnp.sum(prod[HEAD_DIM:], axis=0, keepdims=True)
        d_t[0] = jnp.zeros(d_t.shape[1:], f32)

    v = value[...]
    low = lax.broadcasted_iota(jnp.int32, v.shape, 1) < HEAD_DIM
    here = pl.ds(pl.multiple_of(step * block, block), block)
    dk, dv = [], []
    for e in range(2):
        v_e = jnp.where(low == (e == 0), v, jnp.zeros_like(v))
        p = probs[e]
        dp = dot(v_e, grad_t[...], ((1,), (0,)))
        ds = (p.astype(f32) * (dp - delta[e : e + 1])).astype(bf16)
        dk.append(dot(ds, query[...], ((1,), (0,))))
        dv.append(dot(p, grad_rows[...], ((1,), (0,))))
        rows = slice(e * HEAD_DIM, (e + 1) * HEAD_DIM)
        d_t[0, rows] += dot(key_t[rows, here], ds, ((1,), (0,)))
    d_key[here] = jnp.where(low, dk[0], dk[1])
    d_value[here] = jnp.where(low, dv[0], dv[1])

    @pl.when(step == pl.num_programs(0) - 1)
    def _():
        scale = HEAD_DIM**-0.5
        d_t[0] = d_t[0] * scale
        d_t[1] = jnp.transpose(d_key[...]) * scale
        d_t[2] = jnp.transpose(d_value[...])
        spot = pl.ds(pl.multiple_of(shift[0], HEAD_DIM // 2), COLS)
        gain_sum = jnp.zeros((1, h.shape[1]), f32)
        bias_sum = jnp.zeros((1, h.shape[1]), f32)
        for t in range(3):
            rows = slice(t * COLS, (t + 1) * COLS)
            part = d_t[t, spot].astype(bf16)
            flat[rows] = part
            s = jnp.sum(part.astype(f32), axis=1, keepdims=True)
            col_sums[rows] = s
            grad_b[rows] = dot(part, h[...], ((1,), (0,)))
            w = w_t[pl.ds(pl.multiple_of(t * PAIR + shift[0], HEAD_DIM // 2), COLS)].astype(f32)
            inner = dot(part, xhat[...], ((1,), (0,)))
            gain_sum += jnp.sum(w * inner, axis=0, keepdims=True)
            bias_sum += jnp.sum(w * s, axis=0, keepdims=True)
        for t in range(TP):
            outgoing[t] = flat[:, t * tokens : (t + 1) * tokens]
        sums[0:1] = gain_sum
        sums[1:2] = bias_sum
        sums[2:8] = jnp.zeros((6, sums.shape[1]), f32)


def pair_back(shift, incoming, query, key_t, value, probs, att_t, h_all, xhat_all, w_t):
    row, width = h_all.shape
    tokens = incoming.shape[2]
    block = 256
    return launch(
        pair_back_kernel,
        (row // block,),
        shift,
        [
            (incoming, whole(incoming.shape)),
            (query, whole((row, PAIR))),
            (key_t, whole((PAIR, row))),
            (value, pl.BlockSpec((block, PAIR), lambda i, _: (i, 0))),
            (probs, pl.BlockSpec((2, block, row), lambda i, _: (0, i, 0))),
            (att_t, whole((PAIR, row))),
            (h_all, whole((row, width))),
            (xhat_all, whole((row, width))),
            (w_t, whole(w_t.shape)),
        ],
        [
            (shaped((3 * COLS, width), f32), whole((3 * COLS, width))),
            (shaped((TP, 3 * COLS, tokens), bf16), whole((TP, 3 * COLS, tokens))),
            (shaped((8, width), f32), whole((8, width))),
            (shaped((3 * COLS, 1), f32), whole((3 * COLS, 1))),
        ],
        [
            pltpu.VMEM((PAIR, row), bf16),
            pltpu.VMEM((row, PAIR), bf16),
            pltpu.VMEM((8, row), f32),
            pltpu.VMEM((3, PAIR, row), f32),
            pltpu.VMEM((row, PAIR), f32),
            pltpu.VMEM((row, PAIR), f32),
            pltpu.VMEM((3 * COLS, row), bf16),
        ],
        6 * 10**9,
        10**7,
    )


def hidden_kernel(
    _,
    att,
    x,
    marks,
    grad_mlp,
    incoming,
    w_proj,
    b_proj,
    gain,
    bias,
    w_one,
    b_one,
    w_two,
    grad_one,
    grad_two,
    grad_proj,
    one_sum,
    proj_sum,
):
    @pl.when(pl.program_id(0) == 0)
    def _():
        grad_one[...] = jnp.zeros_like(grad_one)
        grad_two[...] = jnp.zeros_like(grad_two)
        grad_proj[...] = jnp.zeros_like(grad_proj)
        one_sum[...] = jnp.zeros_like(one_sum)
        proj_sum[...] = jnp.zeros_like(proj_sum)

    branch = dot(att[...], w_proj[...], ((1,), (0,))) + b_proj[...]
    y = x[...].astype(f32) * marks[:, 2:3] + marks[:, 0:1] * branch
    h = (normalize(y)[0] * gain[...] + bias[...]).astype(bf16)
    hidden = dot(h, w_one[...], ((1,), (0,))) + b_one[...]
    gelled, slope = gelu_parts(hidden)
    grad_hidden = (dot(grad_mlp[...], w_two[...], ((1,), (1,))) * slope).astype(bf16)
    grad_one[...] += dot(h, grad_hidden, ((0,), (0,)))
    grad_two[...] += dot(gelled.astype(bf16), grad_mlp[...], ((0,), (0,)))
    one_sum[0:1] += jnp.sum(grad_hidden.astype(f32), axis=0, keepdims=True)
    for t in range(incoming.shape[0]):
        piece = incoming[t, PAIR:]
        tokens = piece.shape[1]
        grad_proj[...] += dot(piece, att[t * tokens : (t + 1) * tokens], ((1,), (0,)))
        proj_sum[...] += jnp.sum(piece.astype(f32), axis=1, keepdims=True)


def hidden_grads(group, att, x, marks, grad_mlp, incoming, w_proj, b_proj, gain, bias, w_one, b_one, w_two):
    row, width = x.shape
    tokens = incoming.shape[2]
    block = 256
    tall = pl.BlockSpec((block, width), lambda i, _: (i, 0))
    rows_in = PAIR + COLS
    return launch(
        hidden_kernel,
        (row // block,),
        group,
        [
            (att, tall),
            (x, tall),
            (marks, pl.BlockSpec((block, marks.shape[1]), lambda i, _: (i, 0))),
            (grad_mlp, tall),
            (incoming, pl.BlockSpec((block // tokens, rows_in, tokens), lambda i, _: (i, 0, 0))),
            (w_proj, whole((width, width))),
            (line(b_proj), whole((1, width))),
            (line(gain), whole((1, width))),
            (line(bias), whole((1, width))),
            (w_one, pl.BlockSpec((width, HID), lambda i, g: (0, g[0]))),
            (line(b_one), pl.BlockSpec((1, HID), lambda i, g: (0, g[0]))),
            (w_two, pl.BlockSpec((HID, width), lambda i, g: (g[0], 0))),
        ],
        [
            (shaped((width, HID), f32), whole((width, HID))),
            (shaped((HID, width), f32), whole((HID, width))),
            (shaped((COLS, width), f32), whole((COLS, width))),
            (shaped((8, HID), f32), whole((8, HID))),
            (shaped((COLS, 1), f32), whole((COLS, 1))),
        ],
        [],
        4 * 10**9,
        10**7,
    )


def input_kernel(_, incoming, w_qkv, x, marks, grad_mid, gain, out, flat):
    width = x.shape[1]
    for j in range(TP):
        for t in range(3):
            flat[t * width + j * COLS : t * width + (j + 1) * COLS] = incoming[
                j, t * COLS : (t + 1) * COLS
            ]
    grad_h = jnp.transpose(dot(w_qkv[...], flat[...], ((1,), (0,))))
    valid = marks[:, 2:3]
    normed, inverse = normalize(x[...].astype(f32) * valid)
    back, _gain_sum, _bias_sum = norm_back(grad_h, normed, inverse, gain[...])
    out[...] = ((grad_mid[...] + back) * valid).astype(bf16)


def input_grad(incoming, w_qkv, x, marks, grad_mid, gain):
    tokens, width = x.shape
    tw = whole((tokens, width))
    return launch(
        input_kernel,
        (1,),
        jnp.zeros((1,), jnp.int32),
        [
            (incoming, whole(incoming.shape)),
            (w_qkv, whole(w_qkv.shape)),
            (x, tw),
            (marks, whole(marks.shape)),
            (grad_mid, tw),
            (line(gain), whole((1, width))),
        ],
        [(shaped((tokens, width), bf16), tw)],
        [pltpu.VMEM((3 * width, tokens), bf16)],
        10**9,
        5 * 10**6,
    )[0]


def place_kernel(tasks, n_arrays, n_old, at, *refs):
    arrays = refs[:n_arrays]
    one, two, qkv, proj, raw, wide, split, tall, sem_in, sem_out = refs[n_arrays + n_old :]
    core = at[3]
    first, second = 1 + 2 * core, 3 - 2 * core

    def load(i):
        _, array, entry, _, _ = tasks[i]
        return pltpu.make_async_copy(arrays[array].at[entry], raw.at[i % 2], sem_in.at[i % 2])

    def store(i, begin):
        part, _, _, hop, swapped = tasks[i]
        slot = i % 2
        hops = (0, second if swapped else first, first if swapped else second, 2)
        spot = at[part] ^ hops[hop]
        rows = pl.ds(pl.multiple_of((1 - core if swapped else core) * HID, HID), HID)
        done = sem_out.at[slot]

        def go(source, target):
            copy = pltpu.make_async_copy(source, target, done)
            if begin:
                copy.start()
            else:
                copy.wait()

        columns = pl.ds(pl.multiple_of(spot * D, D), D)
        if part == 0:
            go(wide.at[slot], one.at[rows, columns])
        elif part == 1:
            go(split.at[slot], two.at[:, spot % 2, spot // 2, :, rows])
        else:

            @pl.when(spot < 3)
            def _():
                go(wide.at[slot], qkv.at[rows, columns])

            @pl.when(spot == 3)
            def _():
                go(wide.at[slot], proj.at[rows, :])

    load(0).start()
    for i in range(len(tasks)):
        part = tasks[i][0]
        slot = i % 2
        if i + 1 < len(tasks):
            load(i + 1).start()
        load(i).wait()
        if i >= 2:
            store(i - 2, False)
        high = PIECE[1]
        for a in range(PIECE[0]):
            piece = raw[slot, a].astype(f32)
            if part == 0:
                wide[slot, a // 2 * high : a // 2 * high + high, a % 2 * HID : a % 2 * HID + HID] = piece
            elif part == 1:
                split[slot, a % 4, a // 4 * high : a // 4 * high + high] = piece
            else:
                start = (a % TP) * COLS + a // TP * high
                tall[start : start + high] = piece
        if part == 2:
            wide[slot] = jnp.transpose(tall[...])
        store(i, True)
    for i in range(max(0, len(tasks) - 2), len(tasks)):
        store(i, False)


def place_pieces(at, pieces, old):
    tasks, arrays = [], []
    for part, mine, other, hops in pieces:
        for swapped, array in ((False, mine), (True, other)):
            for entry, hop in enumerate(hops):
                tasks.append((part, len(arrays), entry, hop, swapped))
            arrays.append(array)
    shapes = [
        shaped((D, FF), f32),
        shaped((4, 2, 2, HID // 2, D), f32),
        shaped((D, 3 * D), f32),
        shaped((D, D), f32),
    ]
    anywhere = pl.BlockSpec(memory_space=pl.ANY)
    n_old = len(old)

    def body(*refs):
        place_kernel(tasks, len(arrays), n_old, *refs)

    return pl.pallas_call(
        body,
        grid_spec=pltpu.PrefetchScalarGridSpec(
            num_scalar_prefetch=1,
            grid=(1,),
            in_specs=[anywhere] * (len(arrays) + n_old),
            out_specs=[anywhere] * 4,
            scratch_shapes=[
                pltpu.VMEM((2,) + PIECE, bf16),
                pltpu.VMEM((2, HID, D), f32),
                pltpu.VMEM((2, 4, HID // 2, HID), f32),
                pltpu.VMEM((D, HID), f32),
                pltpu.SemaphoreType.DMA((2,)),
                pltpu.SemaphoreType.DMA((2,)),
            ],
        ),
        out_shape=shapes,
        input_output_aliases={1 + len(arrays) + i: i for i in range(n_old)},
        compiler_params=pltpu.CompilerParams(vmem_limit_bytes=56 * 1024 * 1024),
        cost_estimate=pl.CostEstimate(
            flops=0, bytes_accessed=1800000 * len(tasks), transcendentals=0
        ),
    )(at, *arrays, *old)


def per_device(
    layer_input,
    out_grad,
    lengths,
    keep,
    ln1_gain,
    ln1_bias,
    w_qkv,
    b_query,
    b_value,
    w_proj,
    b_proj,
    ln2_gain,
    ln2_bias,
    w_fc1,
    b_fc1,
    w_fc2,
    b_fc2,
):
    _, tokens, width = layer_input.shape
    row = tokens * TP
    group = lax.axis_index(BLK)
    ends = jnp.cumsum(lengths[0])
    places = jnp.arange(row, dtype=jnp.int32)
    ids = jnp.sum((ends[:, None] <= places[None, :]).astype(jnp.int32), axis=0)
    valid = (ids < IMGS).astype(f32)
    onehot = (ids[:, None] == jnp.arange(IMGS, dtype=jnp.int32)[None, :]).astype(f32)
    keeps = jnp.sum(onehot[None] * keep[:, 0, None, :].astype(f32), axis=2) * drop_scale
    here = group * tokens

    def own(v):
        return lax.dynamic_slice_in_dim(v, here, tokens, 0)


    x_all = spread(layer_input[0], BLK, TP).reshape(row, width)
    marks_all = jnp.stack([keeps[0], keeps[1], valid], axis=1)
    marks = own(marks_all)
    grad_mlp = (marks[:, 1:2] * out_grad[0].astype(f32)).astype(bf16)
    grad_mlp_all = spread(grad_mlp, BLK, TP).reshape(row, width)
    start = first_head(group) * HEAD_DIM
    shift = (group % 2) * (HEAD_DIM // 2)
    w_pair = jnp.concatenate(
        [lax.dynamic_slice(w_qkv, (0, t * width + start), (width, PAIR)) for t in range(3)], axis=1
    )
    bias_pair = jnp.concatenate(
        [
            lax.dynamic_slice_in_dim(b_query, start, PAIR, 0),
            jnp.zeros((PAIR,), f32),
            lax.dynamic_slice_in_dim(b_value, start, PAIR, 0),
        ]
    )
    w_pair_t = jnp.transpose(w_pair)

    attended, h_all, xhat_all = attend(
        here[None], x_all, ids, ln1_gain, ln1_bias, w_qkv, b_query, b_value, tokens
    )
    attended_all = spread(attended, BLK, TP).reshape(row, width)
    output, grad_mid, outgoing, sums_two = mlp(
        attended,
        layer_input[0],
        marks,
        out_grad[0],
        w_proj,
        b_proj,
        ln2_gain,
        ln2_bias,
        w_fc1,
        b_fc1,
        w_fc2,
        b_fc2,
    )
    incoming = lax.all_to_all(outgoing, BLK, 0, 0)
    pair = pair_forward(h_all, w_pair, bias_pair, ids)
    grad_qkv, back_out, sums_one, col_sums = pair_back(
        shift[None], incoming, *pair, h_all, xhat_all, w_pair_t
    )
    back_in = lax.all_to_all(back_out, BLK, 0, 0)
    grad_one, grad_two, grad_proj, one_sum, proj_sum = hidden_grads(
        group[None],
        attended_all,
        x_all,
        marks_all,
        grad_mlp_all,
        incoming,
        w_proj,
        b_proj,
        ln2_gain,
        ln2_bias,
        w_fc1,
        b_fc1,
        w_fc2,
    )
    x_grad = input_grad(back_in, w_qkv, layer_input[0], marks, grad_mid, ln1_gain)
    grad_b = jnp.concatenate([grad_qkv, grad_proj])

    vec = jnp.concatenate(
        [
            sums_one[0],
            sums_one[1],
            sums_two[0],
            sums_two[1],
            sums_two[2],
            one_sum[0],
            col_sums[:COLS, 0],
            col_sums[2 * COLS :, 0],
            proj_sum[:, 0],
            jnp.zeros((VEC_ROWS * HID - 11 * HID - 3 * COLS,), f32),
        ]
    ).reshape(VEC_ROWS, HID)

    def halves(m):
        return jnp.concatenate([m[:, :HID], m[:, HID:]], axis=0)

    ordered_b = jnp.transpose(grad_b.reshape(4, 2, HID // 8, D), (1, 0, 2, 3)).reshape(HID, D)
    piece_one = sum_rows(grad_one, None)
    piece_two = sum_rows(halves(grad_two), None)
    piece_b = sum_rows(halves(ordered_b), vec)
    early_one = spread(piece_one, ("yh", "z", "yl"), 16)
    early_two = spread(piece_two, ("z", "x"), 16)
    early_b = spread(piece_b, ("yh", "x", "yl"), 16)
    vec_all = early_b.reshape(2, TP, HID // 8 + VEC_ROWS, HID)[0, :, HID // 8 :].astype(f32)
    early_b = early_b[:, : HID // 8]
    at = jnp.stack(
        [lax.axis_index("x"), lax.axis_index(("yh", "yl")), lax.axis_index("z"), lax.axis_index("c")]
    ).astype(jnp.int32)
    axes = (("c", "x"), ("yh", "c", "yl"), ("z", "c"))
    parts = (early_one, early_two, early_b)
    near = [exchange(p, axis, (1, 3)) for p, axis in zip(parts, axes)]
    both = [jnp.stack([p, n]) for p, n in zip(parts, near)]
    far = [exchange(b, axis, (3, 1)) for b, axis in zip(both, axes)]
    outs = ()
    for stage, hops in (([p[None] for p in parts], (0,)), ([n[None] for n in near], (1,)), (far, (2, 3))):
        outs = place_pieces(
            at, [(i, p, swap_core(p), hops) for i, p in enumerate(stage)], tuple(outs)
        )
    grad_w_fc1, grad_w_fc2, grad_w_qkv, grad_w_proj = outs
    flat = vec_all.reshape(TP, VEC_ROWS * HID)
    shared = jnp.sum(flat[:, : 5 * D], axis=0).reshape(5, D)
    tail = flat[:, 5 * D + HID :]
    return (
        output[None],
        x_grad[None],
        shared[0],
        shared[1],
        grad_w_qkv,
        tail[:, :COLS].reshape(D),
        tail[:, COLS : 2 * COLS].reshape(D),
        grad_w_proj,
        tail[:, 2 * COLS : 3 * COLS].reshape(D),
        shared[2],
        shared[3],
        grad_w_fc1,
        flat[:, 5 * D : 5 * D + HID].reshape(FF),
        grad_w_fc2.reshape(FF, D),
        shared[4],
    )


def solution(mesh):
    fine = Mesh(mesh.devices.reshape(2, 4, 2, 4, 2), ("yh", "z", "c", "x", "yl"))
    dp = ("yh", "z", "c")
    tokens = P(dp, BLK, None)
    placed = (tokens, tokens, P(dp, None), P(None, dp, None)) + (P(),) * 13
    return jax.shard_map(
        per_device,
        mesh=fine,
        in_specs=placed,
        out_specs=(tokens, tokens) + (P(),) * 13,
        check_vma=False,
    )
```

time: 460 us -> 309 us (0.67)
  the two profiles are of different devices: /device:TPU:17 before, /device:TPU:1 now
where the time goes in v2:
time: 309 us; the launch traced here: 307 us
  Pallas kernels  91.8 us (30%)
  starting transfers between devices  84.9 us (27%)
  waiting for transfers between devices  76.8 us (25%)
  local copies, waits for them, and re-layouts  36.5 us (12%)
  other arithmetic  15.3 us (5%)
    pallas_call x6, Pallas kernels, launch(): pl.pallas_call(body, grid_spec=pltpu.PrefetchScalarGridSpec(num_scalar_pr...  66.9 us
    all_to_all x6, waiting for transfers between devices, spread(): return lax.all_to_all(tiled, axes, 0, 0)  46.1 us
    ppermute x12, starting transfers between devices, swap_core(): return lax.ppermute(block, 'c', [(0, 1), (1, 0)])  28.3 us
    all_to_all x6, starting transfers between devices, spread(): return lax.all_to_all(tiled, axes, 0, 0)  25.3 us
    pallas_call x3, Pallas kernels, place_pieces(): pl.pallas_call(body, grid_spec=pltpu.PrefetchScalarGridSpec(num_scalar_pr...  24.9 us
    all_to_all x3, waiting for transfers between devices, sum_rows(): pieces = lax.all_to_all(pieces, ('yh', 'z'), 0, 0)  19.9 us
    all_to_all x3, starting transfers between devices, sum_rows(): pieces = lax.all_to_all(pieces, ('yh', 'z'), 0, 0)  14.5 us
    ppermute x6, starting transfers between devices, exchange(): return lax.ppermute(block, axis, route)  8.23 us
  transfers between devices with their start and end apart: 29, of which 9 were waited for; matrix products, arithmetic and copies ran while one was open for 13% of the time, Pallas kernels for 22%

profile of v2, /device:TPU:1, one launch (start us, length us, event | category | flops | bytes accessed | tf_op | source)
XLA Modules:
  0.0 306.8 jit_solution(13612442792961750264)
XLA Ops:
  0.6 2.2 broadcast_in_dim.34
  2.8 6.0 %all-to-all-start = ((bf16[8,128,768]{2,1,0:T(8,128)(2,1)}), bf16[8,128,768]{2,1,0:T(8,128)(2,1)S(1)}, u32[]{:S(2)}, u32[]{:S(2)}) async-start(bf16[8,128,768]{2,1,0:T(8,128)(2,1)} %broadcast_in_dim.34), calls=%async_computation | async-start | bytes 3145728 | tf_op jit(solution)/shard_map/all_to_all | solution.py:57
  9.9 22.0 %all-to-all-done = bf16[8,128,768]{2,1,0:T(8,128)(2,1)S(1)} async-done(((bf16[8,128,768]{2,1,0:T(8,128)(2,1)}), bf16[8,128,768]{2,1,0:T(8,128)(2,1)S(1)}, u32[]{:S(2)}, u32[]{:S(2)}) %all-to-all-start) | async-done | bytes 1572896 | tf_op jit(solution)/shard_map/all_to_all | solution.py:57
  31.9 1.3 broadcast_in_dim.42
  33.5 3.6 %all-to-all-start.4 = ((bf16[8,128,768]{2,1,0:T(8,128)(2,1)}), bf16[8,128,768]{2,1,0:T(8,128)(2,1)S(1)}, u32[]{:S(2)}, u32[]{:S(2)}) async-start(bf16[8,128,768]{2,1,0:T(8,128)(2,1)} %broadcast_in_dim.42), calls=%async_computation.4 | async-start | bytes 3145728 | tf_op jit(solution)/shard_map/all_to_all | solution.py:57
  37.1 1.0 copy.63.ids_col
  42.8 1.5 constant_dynamic-slice_fusion.3.marks
  44.3 16.3 %shard_map.280 = (bf16[128,768]{1,0:T(8,128)(2,1)}, bf16[1024,768]{1,0:T(8,128)(2,1)}, bf16[1024,768]{1,0:T(8,128)(2,1)}) custom-call(s32[1]{0:T(128)} %bitcast.at, bf16[1024,768]{1,0:T(8,128)(2,1)} %bitcast.68, s32[1024,1]{1,0:T(8,128)} %copy.63.ids_col, s32[1,1024]{1,0:T(1,128)} %bitcast.104, f32[1,768]{1,0:T(1,128)} %reshape.214.gain, ...), custom_call_target="tpu_custom_call" | custom-call | flops 6000000000 | bytes 10000000 | tf_op jit(solution)/shard_map/pallas_call | solution.py:122
  60.6 11.6 %shard_map.281 = (bf16[128,768]{1,0:T(8,128)(2,1)}, f32[128,768]{1,0:T(8,128)}, bf16[8,224,128]{2,1,0:T(8,128)(2,1)}, f32[8,768]{1,0:T(8,128)}) custom-call(s32[1]{0:T(128)} %constant.76.clone.1._, bf16[128,768]{1,0:T(8,128)(2,1)} %get-tuple-element.48.att, bf16[128,768]{1,0:T(8,128)(2,1)} %bitcast.92, f32[128,3]{1,0:T(8,128)} %constant_dynamic-slice_fusion.3.marks, ...), custom_call_target="tpu_custom_call" | custom-call | flops 3000000000 | bytes 11000000 | tf_op jit(solution)/shard_map/pallas_call | solution.py:122
  72.2 5.1 %all-to-all-start.1 = ((bf16[8,224,128]{2,1,0:T(8,128)(2,1)}), bf16[8,224,128]{2,1,0:T(8,128)(2,1)S(1)}, u32[]{:S(2)}, u32[]{:S(2)}) async-start(bf16[8,224,128]{2,1,0:T(8,128)(2,1)} %get-tuple-element.50), calls=%async_computation.1 | async-start | bytes 917504 | tf_op jit(solution)/shard_map/all_to_all | solution.py:801
  77.5 1.5 constant_dynamic-slice_fusion.2
  79.4 4.6 %all-to-all-done.1.incoming = bf16[8,224,128]{2,1,0:T(8,128)(2,1)S(1)} async-done(((bf16[8,224,128]{2,1,0:T(8,128)(2,1)}), bf16[8,224,128]{2,1,0:T(8,128)(2,1)S(1)}, u32[]{:S(2)}, u32[]{:S(2)}) %all-to-all-start.1) | async-done | bytes 458784 | tf_op jit(solution)/shard_map/all_to_all | solution.py:801
  84.0 1.3 broadcast_in_dim.40
  85.3 3.8 %all-to-all-start.3 = ((bf16[8,128,768]{2,1,0:T(8,128)(2,1)}), bf16[8,128,768]{2,1,0:T(8,128)(2,1)S(1)}, u32[]{:S(2)}, u32[]{:S(2)}) async-start(bf16[8,128,768]{2,1,0:T(8,128)(2,1)} %broadcast_in_dim.40), calls=%async_computation.3 | async-start | bytes 3145728 | tf_op jit(solution)/shard_map/all_to_all | solution.py:57
  89.1 0.9 fusion.8
  90.0 1.1 copy.68.w
  91.6 1.5 slice_reduce_fusion.3
  93.1 11.7 %shard_map.282 = (bf16[1024,128]{1,0:T(8,128)(2,1)}, bf16[128,1024]{1,0:T(8,128)(2,1)}, bf16[1024,128]{1,0:T(8,128)(2,1)}, bf16[2,1024,1024]{2,1,0:T(8,128)(2,1)}, f32[128,1024]{1,0:T(8,128)}) custom-call(s32[1]{0:T(128)} %constant.76.clone.1._, bf16[1024,768]{1,0:T(8,128)(2,1)} %get-tuple-element.51.h, bf16[768,384]{1,0:T(8,128)(2,1)} %copy.68.w, ...), custom_call_target="tpu_custom_call" | custom-call | flops 3000000000 | bytes 8000000 | tf_op jit(solution)/shard_map/pallas_call | solution.py:122
  104.8 11.0 %shard_map.283 = (f32[288,768]{1,0:T(8,128)}, bf16[8,288,128]{2,1,0:T(8,128)(2,1)}, f32[8,768]{1,0:T(8,128)}, f32[288,1]{1,0:T(8,128)}) custom-call(s32[1]{0:T(128)} %bitcast.13.shift, bf16[8,224,128]{2,1,0:T(8,128)(2,1)} %copy-done.11, bf16[1024,128]{1,0:T(8,128)(2,1)} %get-tuple-element.52.query, bf16[128,1024]{1,0:T(8,128)(2,1)} %get-tuple-element.53.key_t, ...), custom_call_target="tpu_custom_call" | custom-call | flops 6000000000 | bytes 10000000 | tf_op jit(solution)/shard_map/pallas_call | solution.py:122
  115.8 0.8 slice_reduce_fusion.6
  116.6 1.5 slice_reduce_fusion.1
  118.1 1.1 copy-done.2
  119.3 11.8 %shard_map.285 = (f32[768,384]{1,0:T(8,128)}, f32[384,768]{1,0:T(8,128)}, f32[96,768]{1,0:T(8,128)}, f32[8,384]{1,0:T(8,128)}, f32[96,1]{1,0:T(8,128)}) custom-call(s32[1]{0:T(128)} %bitcast.16._, bf16[1024,768]{1,0:T(8,128)(2,1)} %bitcast.71, bf16[1024,768]{1,0:T(8,128)(2,1)} %bitcast.69, f32[1024,3]{1,0:T(8,128)} %copy-done.6, bf16[1024,768]{1,0:T(8,128)(2,1)} %bitcast.70, ...), custom_call_target="tpu_custom_call" | custom-call | flops 4000000000 | bytes 10000000 | tf_op jit(solution)/shard_map/pallas_call | solution.py:122
  131.1 1.3 fusion.9
  133.3 3.3 %collective-permute-start.5 = (bf16[384,384]{1,0:T(8,128)(2,1)}, bf16[384,384]{1,0:T(8,128)(2,1)}, u32[]{:S(2)}, u32[]{:S(2)}) collective-permute-start(bf16[384,384]{1,0:T(8,128)(2,1)} %fusion.5), channel_id=1, source_target_pairs={{0,8},{8,0},{1,9},{9,1},{2,10},{10,2},{3,11},{11,3},{4,12},{12,4},... | collective-permute-start | bytes 884744 | tf_op jit(solution)/shard_map/ppermute | solution.py:81
  138.2 1.3 slice_reduce_fusion.8
  139.5 1.4 reduce.12
  141.0 1.4 concatenate.32
  142.4 1.3 reshape.229
  145.3 1.7 fusion.1
  147.0 7.4 %all-to-all-start.9 = ((bf16[8,48,384]{2,1,0:T(8,128)(2,1)}), bf16[8,48,384]{2,1,0:T(8,128)(2,1)S(1)}, u32[]{:S(2)}, u32[]{:S(2)}) async-start(bf16[8,48,384]{2,1,0:T(8,128)(2,1)} %bitcast.42), calls=%async_computation.9 | async-start | bytes 589824 | tf_op jit(solution)/shard_map/all_to_all | solution.py:98
  154.4 1.7 fusion.2
  156.2 5.9 %all-to-all-done.9 = bf16[8,48,384]{2,1,0:T(8,128)(2,1)S(1)} async-done(((bf16[8,48,384]{2,1,0:T(8,128)(2,1)}), bf16[8,48,384]{2,1,0:T(8,128)(2,1)S(1)}, u32[]{:S(2)}, u32[]{:S(2)}) %all-to-all-start.9) | async-done | bytes 294944 | tf_op jit(solution)/shard_map/all_to_all | solution.py:98
  162.1 3.6 %all-to-all-start.7 = ((bf16[8,48,384]{2,1,0:T(8,128)(2,1)}), bf16[8,48,384]{2,1,0:T(8,128)(2,1)S(1)}, u32[]{:S(2)}, u32[]{:S(2)}) async-start(bf16[8,48,384]{2,1,0:T(8,128)(2,1)} %bitcast.36), calls=%async_computation.7 | async-start | bytes 589824 | tf_op jit(solution)/shard_map/all_to_all | solution.py:98
  165.8 1.0 fusion
  167.6 5.9 %all-to-all-done.7 = bf16[8,48,384]{2,1,0:T(8,128)(2,1)S(1)} async-done(((bf16[8,48,384]{2,1,0:T(8,128)(2,1)}), bf16[8,48,384]{2,1,0:T(8,128)(2,1)S(1)}, u32[]{:S(2)}, u32[]{:S(2)}) %all-to-all-start.7) | async-done | bytes 294944 | tf_op jit(solution)/shard_map/all_to_all | solution.py:98
  173.6 3.5 %all-to-all-start.5 = ((bf16[8,64,384]{2,1,0:T(8,128)(2,1)}), bf16[8,64,384]{2,1,0:T(8,128)(2,1)S(1)}, u32[]{:S(2)}, u32[]{:S(2)}) async-start(bf16[8,64,384]{2,1,0:T(8,128)(2,1)} %pad_maximum_fusion.7), calls=%async_computation.5 | async-start | bytes 786432 | tf_op jit(solution)/shard_map/all_to_all | solution.py:98
  177.1 8.1 %all-to-all-done.5 = bf16[8,64,384]{2,1,0:T(8,128)(2,1)S(1)} async-done(((bf16[8,64,384]{2,1,0:T(8,128)(2,1)}), bf16[8,64,384]{2,1,0:T(8,128)(2,1)S(1)}, u32[]{:S(2)}, u32[]{:S(2)}) %all-to-all-start.5) | async-done | bytes 393248 | tf_op jit(solution)/shard_map/all_to_all | solution.py:98
  185.2 0.9 broadcast_in_dim.92
  186.0 4.8 %all-to-all-start.10 = ((bf16[16,48,384]{2,1,0:T(8,128)(2,1)}), bf16[16,48,384]{2,1,0:T(8,128)(2,1)S(1)}, u32[]{:S(2)}, u32[]{:S(2)}) async-start(bf16[16,48,384]{2,1,0:T(8,128)(2,1)} %broadcast_in_dim.92), calls=%async_computation.10 | async-start | bytes 1179648 | tf_op jit(solution)/shard_map/all_to_all | solution.py:57
  190.9 9.4 %all-to-all-done.10 = bf16[16,48,384]{2,1,0:T(8,128)(2,1)S(1)} async-done(((bf16[16,48,384]{2,1,0:T(8,128)(2,1)}), bf16[16,48,384]{2,1,0:T(8,128)(2,1)S(1)}, u32[]{:S(2)}, u32[]{:S(2)}) %all-to-all-start.10) | async-done | bytes 589856 | tf_op jit(solution)/shard_map/all_to_all | solution.py:57
  200.3 1.0 broadcast_in_dim.91
  201.2 3.6 %all-to-all-start.8 = ((bf16[16,48,384]{2,1,0:T(8,128)(2,1)}), bf16[16,48,384]{2,1,0:T(8,128)(2,1)S(1)}, u32[]{:S(2)}, u32[]{:S(2)}) async-start(bf16[16,48,384]{2,1,0:T(8,128)(2,1)} %broadcast_in_dim.91), calls=%async_computation.8 | async-start | bytes 1179648 | tf_op jit(solution)/shard_map/all_to_all | solution.py:57
  204.9 9.2 %all-to-all-done.8 = bf16[16,48,384]{2,1,0:T(8,128)(2,1)S(1)} async-done(((bf16[16,48,384]{2,1,0:T(8,128)(2,1)}), bf16[16,48,384]{2,1,0:T(8,128)(2,1)S(1)}, u32[]{:S(2)}, u32[]{:S(2)}) %all-to-all-start.8) | async-done | bytes 589856 | tf_op jit(solution)/shard_map/all_to_all | solution.py:57
  214.1 1.1 broadcast_in_dim.90
  215.2 3.6 %all-to-all-start.6 = ((bf16[16,64,384]{2,1,0:T(8,128)(2,1)}), bf16[16,64,384]{2,1,0:T(8,128)(2,1)S(1)}, u32[]{:S(2)}, u32[]{:S(2)}) async-start(bf16[16,64,384]{2,1,0:T(8,128)(2,1)} %broadcast_in_dim.90), calls=%async_computation.6 | async-start | bytes 1572864 | tf_op jit(solution)/shard_map/all_to_all | solution.py:57
  218.8 2.5 collective-permute-start.6
  221.3 2.4 collective-permute-start.2
  223.8 5.5 %all-to-all-done.6 = bf16[16,64,384]{2,1,0:T(8,128)(2,1)S(1)} async-done(((bf16[16,64,384]{2,1,0:T(8,128)(2,1)}), bf16[16,64,384]{2,1,0:T(8,128)(2,1)S(1)}, u32[]{:S(2)}, u32[]{:S(2)}) %all-to-all-start.6) | async-done | bytes 786464 | tf_op jit(solution)/shard_map/all_to_all | solution.py:57
  229.3 1.2 collective-permute-start.9
  230.5 6.2 %collective-permute-done.6 = bf16[16,48,384]{2,1,0:T(8,128)(2,1)S(1)} collective-permute-done((bf16[16,48,384]{2,1,0:T(8,128)(2,1)S(1)}, bf16[16,48,384]{2,1,0:T(8,128)(2,1)S(1)}, u32[]{:S(2)}, u32[]{:S(2)}) %collective-permute-start.6) | collective-permute-done | bytes 589856 | tf_op jit(solution)/shard_map/ppermute | solution.py:77
  236.7 1.2 pad_maximum_fusion.4
  238.3 2.2 pad_maximum_fusion.2
  240.5 1.7 collective-permute-start.3
  242.2 1.2 pad_maximum_fusion.5
  243.5 10.8 %collective-permute-start.16 = (bf16[1,16,48,384]{3,2,1,0:T(8,128)(2,1)S(1)}, bf16[1,16,48,384]{3,2,1,0:T(8,128)(2,1)}, u32[]{:S(2)}, u32[]{:S(2)}) collective-permute-start(bf16[1,16,48,384]{3,2,1,0:T(8,128)(2,1)S(1)} %bitcast.73), channel_id=1, source_target_pairs={{0,8},{8,0},{1,9},{9,1},{2,10},{10,2},{3,11},{11,3},{4,12},{12,4},... | collective-permute-start | bytes 1769480 | tf_op jit(solution)/shard_map/ppermute | solution.py:81
  254.4 3.5 %all-to-all-start.2 = ((bf16[8,288,128]{2,1,0:T(8,128)(2,1)}), bf16[8,288,128]{2,1,0:T(8,128)(2,1)S(1)}, u32[]{:S(2)}, u32[]{:S(2)}) async-start(bf16[8,288,128]{2,1,0:T(8,128)(2,1)} %get-tuple-element.58), calls=%async_computation.2 | async-start | bytes 1179648 | tf_op jit(solution)/shard_map/all_to_all | solution.py:806
  258.9 5.3 %collective-permute-start.4 = (bf16[2,16,48,384]{3,2,1,0:T(8,128)(2,1)}, bf16[2,16,48,384]{3,2,1,0:T(8,128)(2,1)}, u32[]{:S(2)}, u32[]{:S(2)}) collective-permute-start(bf16[2,16,48,384]{3,2,1,0:T(8,128)(2,1)} %collective-permute-done.3.refs_1_), channel_id=1, source_target_pairs={{0,8},{8,0},{1,9},{9,1},{2,10},{10,2},{3,11},{11,3},{4,12},{12,4},... | collective-permute-start | bytes 3538952 | tf_op jit(solution)/shard_map/ppermute | solution.py:81
  264.2 6.7 %collective-permute-start.11 = (bf16[2,16,48,384]{3,2,1,0:T(8,128)(2,1)}, bf16[2,16,48,384]{3,2,1,0:T(8,128)(2,1)}, u32[]{:S(2)}, u32[]{:S(2)}) collective-permute-start(bf16[2,16,48,384]{3,2,1,0:T(8,128)(2,1)} %collective-permute-done.10.refs_5_), channel_id=1, source_target_pairs={{0,8},{8,0},{1,9},{9,1},{2,10},{10,2},{3,11},{11,3},{4,12},{12,4},... | collective-permute-start | bytes 3538952 | tf_op jit(solution)/shard_map/ppermute | solution.py:81
  271.6 0.8 copy-done.7
  272.4 4.4 %shard_map.284 = bf16[128,768]{1,0:T(8,128)(2,1)} custom-call(s32[1]{0:T(128)} %constant.76.clone.1._, bf16[8,288,128]{2,1,0:T(8,128)(2,1)} %copy-done.7, bf16[768,2304]{1,0:T(8,128)(2,1)} %w_qkv.1, bf16[128,768]{1,0:T(8,128)(2,1)} %bitcast.93, f32[128,3]{1,0:T(8,128)} %constant_dynamic-slice_fusion.3.marks, f32[128,768]{1,0:T(8,128)} %get-tuple-element.59.grad_mid, ...), custom_call_target="tpu_custom_call" | custom-call | flops 1000000000 | bytes 5000000 | tf_op jit(solution)/shard_map/pallas_call | solution.py:122
  280.8 6.8 %shard_map.286 = (f32[768,3072]{1,0:T(8,128)}, f32[4,2,2,192,768]{4,3,2,1,0:T(8,128)}, f32[768,2304]{1,0:T(8,128)}, f32[768,768]{1,0:T(8,128)}) custom-call(s32[4]{0:T(128)} %pad_add_fusion.refs_0_, bf16[1,16,48,384]{3,2,1,0:T(8,128)(2,1)} %bitcast.77, bf16[1,16,48,384]{3,2,1,0:T(8,128)(2,1)} %collective-permute-done.15.refs_2_, ...), custom_call_target="tpu_custom_call" | custom-call | bytes 10800000 | tf_op jit(solution)/shard_map/pallas_call | solution.py:705
  288.5 6.8 %shard_map.287 = (f32[768,3072]{1,0:T(8,128)}, f32[4,2,2,192,768]{4,3,2,1,0:T(8,128)}, f32[768,2304]{1,0:T(8,128)}, f32[768,768]{1,0:T(8,128)}) custom-call(s32[4]{0:T(128)} %pad_add_fusion.refs_0_, bf16[1,16,48,384]{3,2,1,0:T(8,128)(2,1)} %bitcast.38.refs_1_, ...), custom_call_target="tpu_custom_call", output_to_operand_aliasing={{0}: (7, {}), {1}: (8, {}), {2}: (9, {}), {3}: (10, {})} | custom-call | bytes 10800000 | tf_op jit(solution)/shard_map/pallas_call | solution.py:705
  295.3 11.3 %shard_map.288 = (f32[768,3072]{1,0:T(8,128)}, f32[4,2,2,192,768]{4,3,2,1,0:T(8,128)}, f32[768,2304]{1,0:T(8,128)}, f32[768,768]{1,0:T(8,128)}) custom-call(s32[4]{0:T(128)} %pad_add_fusion.refs_0_, bf16[2,16,48,384]{3,2,1,0:T(8,128)(2,1)} %collective-permute-done.3.refs_1_, ...), custom_call_target="tpu_custom_call", output_to_operand_aliasing={{0}: (7, {}), {1}: (8, {}), {2}: (9, {}), {3}: (10, {})} | custom-call | bytes 21600000 | tf_op jit(solution)/shard_map/pallas_call | solution.py:705
  (149 shorter events, 19.0 us)
Async XLA Ops:
  2.8 6.0 %copy-start.30 = (s32[1,4]{1,0:T(1,128)S(1)}, s32[1,4]{1,0:T(1,128)}, u32[]{:S(2)}) copy-start(s32[1,4]{1,0:T(1,128)} %param.19) | copy-start | bytes 52
  2.8 6.3 %copy-start.29 = (s32[2,1,4]{2,1,0:T(1,128)S(1)}, s32[2,1,4]{2,1,0:T(1,128)}, u32[]{:S(2)}) copy-start(s32[2,1,4]{2,1,0:T(1,128)} %param.20) | copy-start | bytes 100
  2.8 6.9 %copy-start.14 = (bf16[1,128,768]{2,1,0:T(8,128)(2,1)S(1)}, bf16[1,128,768]{2,1,0:T(8,128)(2,1)}, u32[]{:S(2)}) copy-start(bf16[1,128,768]{2,1,0:T(8,128)(2,1)} %param.18) | copy-start | bytes 589828
  2.8 29.0 %all-to-all-start = ((bf16[8,128,768]{2,1,0:T(8,128)(2,1)}), bf16[8,128,768]{2,1,0:T(8,128)(2,1)S(1)}, u32[]{:S(2)}, u32[]{:S(2)}) async-start(bf16[8,128,768]{2,1,0:T(8,128)(2,1)} %broadcast_in_dim.34), calls=%async_computation | async-start | bytes 3145728 | tf_op jit(solution)/shard_map/all_to_all | solution.py:57
  9.1 28.0 %copy-start.20 = (s32[1024]{0:T(1024)}, s32[1024]{0:T(1024)S(1)}, u32[]{:S(2)}) copy-start(s32[1024]{0:T(1024)S(1)} %convert_reduce_fusion) | copy-start | bytes 12292
  9.5 23.7 %copy-start.6 = (f32[1024,3]{1,0:T(8,128)}, f32[1024,3]{1,0:T(8,128)S(1)}, u32[]{:S(2)}) copy-start(f32[1024,3]{1,0:T(8,128)S(1)} %copy.64.marks) | copy-start | bytes 36868
  31.9 1.7 copy-start
  33.2 5.0 %copy-start.21 = (f32[768]{0:T(1024)S(1)}, f32[768]{0:T(1024)}, u32[]{:S(2)}) copy-start(f32[768]{0:T(1024)} %param.21) | copy-start | bytes 9220
  33.2 5.5 %copy-start.22 = (f32[768]{0:T(1024)S(1)}, f32[768]{0:T(1024)}, u32[]{:S(2)}) copy-start(f32[768]{0:T(1024)} %param.22) | copy-start | bytes 9220
  33.2 6.1 %copy-start.27 = (f32[768]{0:T(1024)S(1)}, f32[768]{0:T(1024)}, u32[]{:S(2)}) copy-start(f32[768]{0:T(1024)} %param.24) | copy-start | bytes 9220
  33.2 6.7 %copy-start.28 = (f32[768]{0:T(1024)S(1)}, f32[768]{0:T(1024)}, u32[]{:S(2)}) copy-start(f32[768]{0:T(1024)} %param.25) | copy-start | bytes 9220
  33.2 7.3 %copy-start.23 = (f32[768]{0:T(1024)S(1)}, f32[768]{0:T(1024)}, u32[]{:S(2)}) copy-start(f32[768]{0:T(1024)} %param.27) | copy-start | bytes 9220
  33.2 7.8 %copy-start.24 = (f32[768]{0:T(1024)S(1)}, f32[768]{0:T(1024)}, u32[]{:S(2)}) copy-start(f32[768]{0:T(1024)} %param.28) | copy-start | bytes 9220
  33.2 8.4 %copy-start.25 = (f32[768]{0:T(1024)S(1)}, f32[768]{0:T(1024)}, u32[]{:S(2)}) copy-start(f32[768]{0:T(1024)} %param.29) | copy-start | bytes 9220
  33.3 9.0 %copy-start.26 = (f32[768]{0:T(1024)S(1)}, f32[768]{0:T(1024)}, u32[]{:S(2)}) copy-start(f32[768]{0:T(1024)} %param.33) | copy-start | bytes 9220
  33.5 38.7 %all-to-all-start.4 = ((bf16[8,128,768]{2,1,0:T(8,128)(2,1)}), bf16[8,128,768]{2,1,0:T(8,128)(2,1)S(1)}, u32[]{:S(2)}, u32[]{:S(2)}) async-start(bf16[8,128,768]{2,1,0:T(8,128)(2,1)} %broadcast_in_dim.42), calls=%async_computation.4 | async-start | bytes 3145728 | tf_op jit(solution)/shard_map/all_to_all | solution.py:57
  72.2 6.9 %copy-start.1 = (bf16[8,128,768]{2,1,0:T(8,128)(2,1)}, bf16[8,128,768]{2,1,0:T(8,128)(2,1)S(1)}, u32[]{:S(2)}) copy-start(bf16[8,128,768]{2,1,0:T(8,128)(2,1)S(1)} %all-to-all-done.4) | copy-start | bytes 4718596
  72.2 11.8 %all-to-all-start.1 = ((bf16[8,224,128]{2,1,0:T(8,128)(2,1)}), bf16[8,224,128]{2,1,0:T(8,128)(2,1)S(1)}, u32[]{:S(2)}, u32[]{:S(2)}) async-start(bf16[8,224,128]{2,1,0:T(8,128)(2,1)} %get-tuple-element.50), calls=%async_computation.1 | async-start | bytes 917504 | tf_op jit(solution)/shard_map/all_to_all | solution.py:801
  77.5 6.5 %copy-start.13 = (bf16[128,768]{1,0:T(8,128)(2,1)S(1)}, bf16[128,768]{1,0:T(8,128)(2,1)}, u32[]{:S(2)}) copy-start(bf16[128,768]{1,0:T(8,128)(2,1)} %get-tuple-element.48.att) | copy-start | bytes 589828
  84.0 1.3 copy-start.11
  85.3 32.8 %all-to-all-start.3 = ((bf16[8,128,768]{2,1,0:T(8,128)(2,1)}), bf16[8,128,768]{2,1,0:T(8,128)(2,1)S(1)}, u32[]{:S(2)}, u32[]{:S(2)}) async-start(bf16[8,128,768]{2,1,0:T(8,128)(2,1)} %broadcast_in_dim.40), calls=%async_computation.3 | async-start | bytes 3145728 | tf_op jit(solution)/shard_map/all_to_all | solution.py:57
  118.1 1.1 copy-start.2
  132.5 4.2 %copy-start.15 = (f32[768,384]{1,0:T(8,128)S(1)}, f32[768,384]{1,0:T(8,128)}, u32[]{:S(2)}) copy-start(f32[768,384]{1,0:T(8,128)} %get-tuple-element.67) | copy-start | bytes 3538948
  132.5 5.4 %copy-start.12 = (f32[288,768]{1,0:T(8,128)S(1)}, f32[288,768]{1,0:T(8,128)}, u32[]{:S(2)}) copy-start(f32[288,768]{1,0:T(8,128)} %get-tuple-element.60) | copy-start | bytes 2654212
  132.6 5.3 %copy-start.18 = (f32[96,768]{1,0:T(8,128)S(1)}, f32[96,768]{1,0:T(8,128)}, u32[]{:S(2)}) copy-start(f32[96,768]{1,0:T(8,128)} %get-tuple-element.61) | copy-start | bytes 884740
  133.3 11.9 %collective-permute-start.5 = (bf16[384,384]{1,0:T(8,128)(2,1)}, bf16[384,384]{1,0:T(8,128)(2,1)}, u32[]{:S(2)}, u32[]{:S(2)}) collective-permute-start(bf16[384,384]{1,0:T(8,128)(2,1)} %fusion.5), channel_id=1, source_target_pairs={{0,8},{8,0},{1,9},{9,1},{2,10},{10,2},{3,11},{11,3},{4,12},{12,4},... | collective-permute-start | bytes 884744 | tf_op jit(solution)/shard_map/ppermute | solution.py:81
  137.4 17.0 %collective-permute-start.1 = (bf16[384,384]{1,0:T(8,128)(2,1)}, bf16[384,384]{1,0:T(8,128)(2,1)}, u32[]{:S(2)}, u32[]{:S(2)}) collective-permute-start(bf16[384,384]{1,0:T(8,128)(2,1)} %fusion.4), channel_id=1, source_target_pairs={{0,8},{8,0},{1,9},{9,1},{2,10},{10,2},{3,11},{11,3},{4,12},{12,4},... | collective-permute-start | bytes 884744 | tf_op jit(solution)/shard_map/ppermute | solution.py:81
  145.3 20.5 %collective-permute-start = (bf16[400,384]{1,0:T(8,128)(2,1)}, bf16[400,384]{1,0:T(8,128)(2,1)}, u32[]{:S(2)}, u32[]{:S(2)}) collective-permute-start(bf16[400,384]{1,0:T(8,128)(2,1)} %pad_maximum_fusion.8), channel_id=1, source_target_pairs={{0,8},{8,0},{1,9},{9,1},{2,10},{10,2},{3,11},{11,3},{4,12},{12,4},... | collective-permute-start | bytes 921608 | tf_op jit(solution)/shard_map/ppermute | solution.py:81
  147.0 15.1 %all-to-all-start.9 = ((bf16[8,48,384]{2,1,0:T(8,128)(2,1)}), bf16[8,48,384]{2,1,0:T(8,128)(2,1)S(1)}, u32[]{:S(2)}, u32[]{:S(2)}) async-start(bf16[8,48,384]{2,1,0:T(8,128)(2,1)} %bitcast.42), calls=%async_computation.9 | async-start | bytes 589824 | tf_op jit(solution)/shard_map/all_to_all | solution.py:98
  154.4 11.3 %copy-start.19 = (f32[16,384]{1,0:T(8,128)S(1)}, f32[16,384]{1,0:T(8,128)}, u32[]{:S(2)}) copy-start(f32[16,384]{1,0:T(8,128)} %reshape.229) | copy-start | bytes 73732
  162.1 11.5 %all-to-all-start.7 = ((bf16[8,48,384]{2,1,0:T(8,128)(2,1)}), bf16[8,48,384]{2,1,0:T(8,128)(2,1)S(1)}, u32[]{:S(2)}, u32[]{:S(2)}) async-start(bf16[8,48,384]{2,1,0:T(8,128)(2,1)} %bitcast.36), calls=%async_computation.7 | async-start | bytes 589824 | tf_op jit(solution)/shard_map/all_to_all | solution.py:98
  173.6 11.6 %all-to-all-start.5 = ((bf16[8,64,384]{2,1,0:T(8,128)(2,1)}), bf16[8,64,384]{2,1,0:T(8,128)(2,1)S(1)}, u32[]{:S(2)}, u32[]{:S(2)}) async-start(bf16[8,64,384]{2,1,0:T(8,128)(2,1)} %pad_maximum_fusion.7), calls=%async_computation.5 | async-start | bytes 786432 | tf_op jit(solution)/shard_map/all_to_all | solution.py:98
  186.0 14.2 %all-to-all-start.10 = ((bf16[16,48,384]{2,1,0:T(8,128)(2,1)}), bf16[16,48,384]{2,1,0:T(8,128)(2,1)S(1)}, u32[]{:S(2)}, u32[]{:S(2)}) async-start(bf16[16,48,384]{2,1,0:T(8,128)(2,1)} %broadcast_in_dim.92), calls=%async_computation.10 | async-start | bytes 1179648 | tf_op jit(solution)/shard_map/all_to_all | solution.py:57
  200.3 43.2 %copy-start.4 = (bf16[16,48,384]{2,1,0:T(8,128)(2,1)}, bf16[16,48,384]{2,1,0:T(8,128)(2,1)S(1)}, u32[]{:S(2)}) copy-start(bf16[16,48,384]{2,1,0:T(8,128)(2,1)S(1)} %all-to-all-done.10) | copy-start | bytes 1769476
  201.2 12.9 %all-to-all-start.8 = ((bf16[16,48,384]{2,1,0:T(8,128)(2,1)}), bf16[16,48,384]{2,1,0:T(8,128)(2,1)S(1)}, u32[]{:S(2)}, u32[]{:S(2)}) async-start(bf16[16,48,384]{2,1,0:T(8,128)(2,1)} %broadcast_in_dim.91), calls=%async_computation.8 | async-start | bytes 1179648 | tf_op jit(solution)/shard_map/all_to_all | solution.py:57
  214.1 40.1 %copy-start.5 = (bf16[16,48,384]{2,1,0:T(8,128)(2,1)}, bf16[16,48,384]{2,1,0:T(8,128)(2,1)S(1)}, u32[]{:S(2)}) copy-start(bf16[16,48,384]{2,1,0:T(8,128)(2,1)S(1)} %all-to-all-done.8) | copy-start | bytes 1769476
  215.2 14.0 %all-to-all-start.6 = ((bf16[16,64,384]{2,1,0:T(8,128)(2,1)}), bf16[16,64,384]{2,1,0:T(8,128)(2,1)S(1)}, u32[]{:S(2)}, u32[]{:S(2)}) async-start(bf16[16,64,384]{2,1,0:T(8,128)(2,1)} %broadcast_in_dim.90), calls=%async_computation.6 | async-start | bytes 1572864 | tf_op jit(solution)/shard_map/all_to_all | solution.py:57
  218.8 17.9 %collective-permute-start.6 = (bf16[16,48,384]{2,1,0:T(8,128)(2,1)S(1)}, bf16[16,48,384]{2,1,0:T(8,128)(2,1)S(1)}, u32[]{:S(2)}, u32[]{:S(2)}) collective-permute-start(bf16[16,48,384]{2,1,0:T(8,128)(2,1)S(1)} %all-to-all-done.10), channel_id=1, source_target_pairs={{0,1},{1,0},{8,73},{9,72},{64,65},{65,64},{72,9},{73,8},{2,3},{3,2... | collective-permute-start | bytes 1769480 | tf_op jit(solution)/shard_map/ppermute | solution.py:77
  221.3 17.0 %collective-permute-start.2 = (bf16[16,48,384]{2,1,0:T(8,128)(2,1)S(1)}, bf16[16,48,384]{2,1,0:T(8,128)(2,1)}, u32[]{:S(2)}, u32[]{:S(2)}) collective-permute-start(bf16[16,48,384]{2,1,0:T(8,128)(2,1)S(1)} %all-to-all-done.8), channel_id=1, source_target_pairs={{0,2},{2,0},{4,6},{6,4},{8,14},{10,12},{12,10},{14,8},{1,3},{3,1},... | collective-permute-start | bytes 1769480 | tf_op jit(solution)/shard_map/ppermute | solution.py:77
  229.3 28.6 %copy-start.3 = (bf16[1,16,48,384]{3,2,1,0:T(8,128)(2,1)}, bf16[1,16,48,384]{3,2,1,0:T(8,128)(2,1)S(1)}, u32[]{:S(2)}) copy-start(bf16[1,16,48,384]{3,2,1,0:T(8,128)(2,1)S(1)} %get-tuple-element.95.refs_5_) | copy-start | bytes 1769476
  229.3 12.9 %collective-permute-start.9 = (bf16[16,48,384]{2,1,0:T(8,128)(2,1)S(1)}, bf16[16,48,384]{2,1,0:T(8,128)(2,1)S(1)}, u32[]{:S(2)}, u32[]{:S(2)}) collective-permute-start(bf16[16,48,384]{2,1,0:T(8,128)(2,1)S(1)} %get-tuple-element.96), channel_id=1, source_target_pairs={{0,16},{8,56},{16,0},{24,40},{32,48},{40,24},{48,32},{56,8},{1,17}... | collective-permute-start | bytes 1769480 | tf_op jit(solution)/shard_map/ppermute | solution.py:77
  236.7 1.2 copy-start.8
  237.9 20.6 %collective-permute-start.7 = (bf16[2,16,48,384]{3,2,1,0:T(8,128)(2,1)}, bf16[2,16,48,384]{3,2,1,0:T(8,128)(2,1)}, u32[]{:S(2)}, u32[]{:S(2)}) collective-permute-start(bf16[2,16,48,384]{3,2,1,0:T(8,128)(2,1)} %pad_maximum_fusion.4), channel_id=1, source_target_pairs={{0,65},{1,64},{8,9},{9,8},{64,1},{65,0},{72,73},{73,72},{2,67},{3,... | collective-permute-start | bytes 3538952 | tf_op jit(solution)/shard_map/ppermute | solution.py:77
  240.5 18.4 %collective-permute-start.3 = (bf16[2,16,48,384]{3,2,1,0:T(8,128)(2,1)}, bf16[2,16,48,384]{3,2,1,0:T(8,128)(2,1)}, u32[]{:S(2)}, u32[]{:S(2)}) collective-permute-start(bf16[2,16,48,384]{3,2,1,0:T(8,128)(2,1)} %pad_maximum_fusion.2), channel_id=1, source_target_pairs={{0,6},{2,4},{4,2},{6,0},{8,10},{10,8},{12,14},{14,12},{1,7},{3,5},... | collective-permute-start | bytes 3538952 | tf_op jit(solution)/shard_map/ppermute | solution.py:77
  242.2 1.2 copy-start.9
  243.4 20.8 %collective-permute-start.10 = (bf16[2,16,48,384]{3,2,1,0:T(8,128)(2,1)}, bf16[2,16,48,384]{3,2,1,0:T(8,128)(2,1)}, u32[]{:S(2)}, u32[]{:S(2)}) collective-permute-start(bf16[2,16,48,384]{3,2,1,0:T(8,128)(2,1)} %pad_maximum_fusion.5), channel_id=1, source_target_pairs={{0,48},{8,24},{16,32},{24,8},{32,16},{40,56},{48,0},{56,40},{1,49}... | collective-permute-start | bytes 3538952 | tf_op jit(solution)/shard_map/ppermute | solution.py:77
  243.5 14.4 %collective-permute-start.16 = (bf16[1,16,48,384]{3,2,1,0:T(8,128)(2,1)S(1)}, bf16[1,16,48,384]{3,2,1,0:T(8,128)(2,1)}, u32[]{:S(2)}, u32[]{:S(2)}) collective-permute-start(bf16[1,16,48,384]{3,2,1,0:T(8,128)(2,1)S(1)} %bitcast.73), channel_id=1, source_target_pairs={{0,8},{8,0},{1,9},{9,1},{2,10},{10,2},{3,11},{11,3},{4,12},{12,4},... | collective-permute-start | bytes 1769480 | tf_op jit(solution)/shard_map/ppermute | solution.py:81
  254.3 4.2 %collective-permute-start.15 = (bf16[1,16,48,384]{3,2,1,0:T(8,128)(2,1)S(1)}, bf16[1,16,48,384]{3,2,1,0:T(8,128)(2,1)}, u32[]{:S(2)}, u32[]{:S(2)}) collective-permute-start(bf16[1,16,48,384]{3,2,1,0:T(8,128)(2,1)S(1)} %bitcast.76), channel_id=1, source_target_pairs={{0,8},{8,0},{1,9},{9,1},{2,10},{10,2},{3,11},{11,3},{4,12},{12,4},... | collective-permute-start | bytes 1769480 | tf_op jit(solution)/shard_map/ppermute | solution.py:81
  254.4 17.2 %all-to-all-start.2 = ((bf16[8,288,128]{2,1,0:T(8,128)(2,1)}), bf16[8,288,128]{2,1,0:T(8,128)(2,1)S(1)}, u32[]{:S(2)}, u32[]{:S(2)}) async-start(bf16[8,288,128]{2,1,0:T(8,128)(2,1)} %get-tuple-element.58), calls=%async_computation.2 | async-start | bytes 1179648 | tf_op jit(solution)/shard_map/all_to_all | solution.py:806
  257.9 18.9 %collective-permute-start.17 = (bf16[1,16,48,384]{3,2,1,0:T(8,128)(2,1)S(1)}, bf16[1,16,48,384]{3,2,1,0:T(8,128)(2,1)}, u32[]{:S(2)}, u32[]{:S(2)}) collective-permute-start(bf16[1,16,48,384]{3,2,1,0:T(8,128)(2,1)S(1)} %get-tuple-element.95.refs_5_), channel_id=1, source_target_pairs={{0,8},{8,0},{1,9},{9,1},{2,10},{10,2},{3,11},{11,3},{4,12},{12,4},... | collective-permute-start | bytes 1769480 | tf_op jit(solution)/shard_map/ppermute | solution.py:81
  258.4 18.4 %collective-permute-start.13 = (bf16[1,16,48,384]{3,2,1,0:T(8,128)(2,1)}, bf16[1,16,48,384]{3,2,1,0:T(8,128)(2,1)S(1)}, u32[]{:S(2)}, u32[]{:S(2)}) collective-permute-start(bf16[1,16,48,384]{3,2,1,0:T(8,128)(2,1)} %bitcast.86), channel_id=1, source_target_pairs={{0,8},{8,0},{1,9},{9,1},{2,10},{10,2},{3,11},{11,3},{4,12},{12,4},... | collective-permute-start | bytes 1769480 | tf_op jit(solution)/shard_map/ppermute | solution.py:81
  258.5 36.8 %collective-permute-start.8 = (bf16[2,16,48,384]{3,2,1,0:T(8,128)(2,1)}, bf16[2,16,48,384]{3,2,1,0:T(8,128)(2,1)}, u32[]{:S(2)}, u32[]{:S(2)}) collective-permute-start(bf16[2,16,48,384]{3,2,1,0:T(8,128)(2,1)} %collective-permute-done.7.refs_3_), channel_id=1, source_target_pairs={{0,8},{8,0},{1,9},{9,1},{2,10},{10,2},{3,11},{11,3},{4,12},{12,4},... | collective-permute-start | bytes 3538952 | tf_op jit(solution)/shard_map/ppermute | solution.py:81
  258.9 36.4 %collective-permute-start.4 = (bf16[2,16,48,384]{3,2,1,0:T(8,128)(2,1)}, bf16[2,16,48,384]{3,2,1,0:T(8,128)(2,1)}, u32[]{:S(2)}, u32[]{:S(2)}) collective-permute-start(bf16[2,16,48,384]{3,2,1,0:T(8,128)(2,1)} %collective-permute-done.3.refs_1_), channel_id=1, source_target_pairs={{0,8},{8,0},{1,9},{9,1},{2,10},{10,2},{3,11},{11,3},{4,12},{12,4},... | collective-permute-start | bytes 3538952 | tf_op jit(solution)/shard_map/ppermute | solution.py:81
  264.2 31.1 %collective-permute-start.11 = (bf16[2,16,48,384]{3,2,1,0:T(8,128)(2,1)}, bf16[2,16,48,384]{3,2,1,0:T(8,128)(2,1)}, u32[]{:S(2)}, u32[]{:S(2)}) collective-permute-start(bf16[2,16,48,384]{3,2,1,0:T(8,128)(2,1)} %collective-permute-done.10.refs_5_), channel_id=1, source_target_pairs={{0,8},{8,0},{1,9},{9,1},{2,10},{10,2},{3,11},{11,3},{4,12},{12,4},... | collective-permute-start | bytes 3538952 | tf_op jit(solution)/shard_map/ppermute | solution.py:81
  271.6 0.8 copy-start.7
  272.4 4.4 %copy-start.10 = (bf16[16,48,384]{2,1,0:T(8,128)(2,1)S(1)}, bf16[16,48,384]{2,1,0:T(8,128)(2,1)}, u32[]{:S(2)}) copy-start(bf16[16,48,384]{2,1,0:T(8,128)(2,1)} %copy-done.9) | copy-start | bytes 1769476
  276.8 10.9 %collective-permute-start.12 = (bf16[1,16,48,384]{3,2,1,0:T(8,128)(2,1)}, bf16[1,16,48,384]{3,2,1,0:T(8,128)(2,1)S(1)}, u32[]{:S(2)}, u32[]{:S(2)}) collective-permute-start(bf16[1,16,48,384]{3,2,1,0:T(8,128)(2,1)} %bitcast.38.refs_1_), channel_id=1, source_target_pairs={{0,8},{8,0},{1,9},{9,1},{2,10},{10,2},{3,11},{11,3},{4,12},{12,4},... | collective-permute-start | bytes 1769480 | tf_op jit(solution)/shard_map/ppermute | solution.py:81
  276.8 10.8 %copy-start.16 = (bf16[1,16,48,384]{3,2,1,0:T(8,128)(2,1)}, bf16[1,16,48,384]{3,2,1,0:T(8,128)(2,1)S(1)}, u32[]{:S(2)}) copy-start(bf16[1,16,48,384]{3,2,1,0:T(8,128)(2,1)S(1)} %collective-permute-done.13.refs_4_) | copy-start | bytes 1769476
  276.8 10.8 %collective-permute-start.14 = (bf16[1,16,48,384]{3,2,1,0:T(8,128)(2,1)S(1)}, bf16[1,16,48,384]{3,2,1,0:T(8,128)(2,1)}, u32[]{:S(2)}, u32[]{:S(2)}) collective-permute-start(bf16[1,16,48,384]{3,2,1,0:T(8,128)(2,1)S(1)} %bitcast.90), channel_id=1, source_target_pairs={{0,8},{8,0},{1,9},{9,1},{2,10},{10,2},{3,11},{11,3},{4,12},{12,4},... | collective-permute-start | bytes 1769480 | tf_op jit(solution)/shard_map/ppermute | solution.py:81
  287.6 0.8 copy-start.17
